TPU v7x, 32 devices: a whole 2x2x4 slice. The times are simulated.
32 devices in a mesh: traj: 2 (over y), pair: 4 (over z), aux: 2 (over x), root: 2 (over core).
Axes of the slice: x: 2, y: 2, z: 4, core: 2. Of those that a mesh axis runs over, the one named last changes fastest.
Arguments:
- b_built: bfloat16 [4, 4, 1024, 2048], P(('traj', 'aux'), None, None, 'pair'), parts along dimension 0, may hold values from -0.0625 to 0.0625
- trial: bfloat16 [16384, 512], P(('traj', 'pair', 'aux'), 'root'), parts along dimension 0, may hold values from -6 to 6
- energy_gap: float32 [16384], P(('traj', 'pair', 'aux')), parts along dimension 0, may hold values from 0.3 to 3
- block_live: int32 [128], P(('traj', 'pair')), parts along dimension 0, may hold values from 0 to 1, as said below
Outputs:
- sigma_out: bfloat16 [16384, 512], P(('traj', 'pair', 'aux'), 'root'), parts along dimension 0
There are 2 independent parts, one for each index of `traj`. A program takes and returns all parts, laid end to end along the dimension named above; each array names one. Nothing has to cross between parts.
Inputs may be any that keep to these rules, and one draw needn't show every extreme that they name: `block_live`: each pair index holds at most 10 screened-in blocks among its 16, one or more, and some pair index holds exactly 10.
All inputs are finite; a program needn't handle non-finite values.
Results may differ from a plain program's by a relative error of at most 0.0045.
Values may be sent and summed in bfloat16 or wider, within the bound.
No kernel may reach another device: no remote copies, remote signals or barrier semaphores. Data moves between devices by JAX's collectives and lax.ppermute only.
A program may use at most 64 MiB of HBM per device.

v0:
```python
import jax
import jax.numpy as jnp
from jax import lax
from jax.sharding import PartitionSpec as P

BLK = 128


def contract_rows(left, right):
    return lax.dot_general(
        left, right, (((0,), (0,)), ((), ())), preferred_element_type=jnp.float32
    )


def body(b_built, trial, energy_gap, block_live):
    slice_rows = trial.shape[0]
    live_rows = jnp.repeat(block_live, BLK)
    offset = lax.axis_index("aux") * slice_rows
    own_live = lax.dynamic_slice_in_dim(live_rows, offset, slice_rows, 0)
    masked = trial * own_live.astype(jnp.bfloat16)[:, None]
    relaid = lax.all_to_all(
        lax.all_to_all(b_built, "pair", split_axis=1, concat_axis=3, tiled=True),
        "aux",
        split_axis=3,
        concat_axis=0,
        tiled=True,
    )
    b_rows = relaid.reshape(-1, relaid.shape[3])
    part_rows = b_rows
    aux_partial = contract_rows(part_rows, lax.all_gather(masked, "aux", axis=0, tiled=True))
    coeffs = lax.psum(aux_partial.astype(jnp.bfloat16), "pair")
    part_rows = b_rows
    response = lax.psum_scatter(
        jnp.dot(part_rows, coeffs, preferred_element_type=jnp.float32).astype(jnp.bfloat16),
        "aux",
        scatter_dimension=0,
        tiled=True,
    ).astype(jnp.float32)
    sigma_out = (
        energy_gap[:, None] * trial.astype(jnp.float32)
        + 2.0 * own_live.astype(jnp.float32)[:, None] * response
    )
    return sigma_out.astype(jnp.bfloat16)


def solution(mesh):
    return jax.shard_map(
        body,
        mesh=mesh,
        in_specs=(
            P(("traj", "aux"), None, None, "pair"),
            P(("traj", "pair", "aux"), "root"),
            P(("traj", "pair", "aux")),
            P(("traj", "pair")),
        ),
        out_specs=P(("traj", "pair", "aux"), "root"),
        check_vma=False,
    )
```

profile of v0, /device:TPU:0, one launch (start us, length us, event | category | flops | bytes accessed | tf_op | source)
XLA Modules:
  0.0 333.2 jit_solution(13828515734199539885)
XLA Ops:
  6.5 0.0 copy-start
  6.5 6.3 %copy.16 = bf16[1,4,1024,512]{2,3,0,1:T(8,128)(2,1)} copy(bf16[1,4,1024,512]{3,2,1,0:T(8,128)(2,1)} %param.4) | data formatting | bytes 8388608 | tf_op args[0]
  12.8 99.5 %all_to_all.33 = bf16[1,4,1024,512]{2,3,0,1:T(8,128)(2,1)S(1)} all-to-all(bf16[1,4,1024,512]{2,3,0,1:T(8,128)(2,1)} %copy.16), channel_id=1, replica_groups=mesh['traj'=2,'pair'=4,'aux'=2,'root'=2] {'pair'}, dimensions={1} | all-to-all | bytes 8388608 | tf_op jit(solution)/shard_map/all_to_all | solution.py:22
  112.3 28.6 %copy.22 = bf16[1,1,1024,2048]{2,1,0,3:T(2,128)(2,1)} copy(bf16[1,1,1024,2048]{2,3,1,0:T(8,128)(2,1)S(1)} %bitcast.25) | data formatting | bytes 8388608 | tf_op jit(solution)/shard_map/all_to_all | solution.py:22
  140.9 0.5 broadcast.4
  141.4 26.0 %reduce = bf16[2048,1024]{1,0:T(8,128)(2,1)} reduce(bf16[2048,1,1,1024]{3,2,1,0:T(2,128)(2,1)} %bitcast.23, bf16[]{:T(256)} %broadcast.4), dimensions={1,2}, to_apply=%bitcast.22.reduce_sub_computation | reduce | bytes 8388610
  167.4 5.9 %reshape.13 = bf16[2,2,524288]{2,1,0:T(2,128)(2,1)} reshape(bf16[2048,1024]{1,0:T(8,128)(2,1)} %reduce) | data formatting | bytes 8388608
  173.3 0.0 copy-start.1
  173.3 5.8 %all-to-all-start.1 = ((bf16[2,2,524288]{2,1,0:T(2,128)(2,1)}), bf16[2,2,524288]{2,1,0:T(2,128)(2,1)}, u32[]{:S(2)}, u32[]{:S(2)}) async-start(bf16[2,2,524288]{2,1,0:T(2,128)(2,1)} %reshape.13), calls=%async_computation.1 | async-start | bytes 8388608 | tf_op jit(solution)/shard_map/all_to_all | solution.py:21
  179.0 0.0 all-gather.2.cloned.1.call-start
  179.1 0.0 copy-done
  179.1 0.1 broadcast_bitcast_fusion
  179.2 0.0 copy-done.1
  179.2 1.0 broadcast_multiply_fusion
  180.2 0.0 all-gather.2.cloned.1.call-update
  180.2 0.0 all-reduce.2.cloned.1.call-start
  180.2 56.5 %all-to-all-done.1 = bf16[2,2,524288]{2,1,0:T(2,128)(2,1)} async-done(((bf16[2,2,524288]{2,1,0:T(2,128)(2,1)}), bf16[2,2,524288]{2,1,0:T(2,128)(2,1)}, u32[]{:S(2)}, u32[]{:S(2)}) %all-to-all-start.1) | async-done | bytes 4194336 | tf_op jit(solution)/shard_map/all_to_all | solution.py:21
  236.8 7.1 %reshape.14 = bf16[2048,1,1,1024]{3,2,1,0:T(2,128)(2,1)} reshape(bf16[2,2,524288]{2,1,0:T(2,128)(2,1)} %all-to-all-done.1) | data formatting | bytes 8388608
  243.9 7.0 %copy.20 = bf16[1,1,1024,2048]{2,3,0,1:T(8,128)(2,1)} copy(bf16[1,1,1024,2048]{2,1,0,3:T(2,128)(2,1)} %bitcast.24) | data formatting | bytes 8388608
  250.9 6.2 %copy.18 = bf16[2,1,1,1024,1024]{4,3,0,2,1:T(8,128)(2,1)} copy(bf16[2,1,1,1024,1024]{3,4,0,2,1:T(8,128)(2,1)} %bitcast.26) | data formatting | bytes 8388608 | tf_op jit(solution)/shard_map/all_to_all | solution.py:21
  257.1 0.0 all-gather.2.cloned.1.call-done
  257.1 4.6 %fusion.1 = bf16[1024,256]{0,1:T(8,128)(2,1)} fusion(bf16[2048,256]{1,0:T(8,128)(2,1)} %all-gather.2.cloned.1.call-done, bf16[2048,1024]{1,0:T(8,128)(2,1)} %bitcast.27), kind=kOutput, calls=%fused_computation.3 | convolution fusion | flops 1074003968 | bytes 5767168 | tf_op jit(solution)/shard_map/dot_general | solution.py:10
  261.7 0.0 all-reduce.2.cloned.1.call-update
  261.8 0.0 copy-start.2
  261.8 0.0 reduce-scatter.2.cloned.1.call-start
  261.8 37.5 %all-reduce.2.cloned.1.call-done = bf16[1024,256]{0,1:T(8,128)(2,1)} async-done(((bf16[1024,256]{0,1:T(8,128)(2,1)}), bf16[1024,256]{0,1:T(8,128)(2,1)}) %all-reduce.2.cloned.1.call-update) | async-done | bytes 524304 | tf_op jit(solution)/shard_map/psum | solution.py:31
  299.3 4.6 %fusion = bf16[2048,256]{0,1:T(8,128)(2,1)} fusion(bf16[1024,256]{0,1:T(8,128)(2,1)} %all-reduce.2.cloned.1.call-done, bf16[2048,1024]{1,0:T(8,128)(2,1)} %bitcast.28), kind=kOutput, calls=%fused_computation.1 | convolution fusion | flops 1074266112 | bytes 5767168 | tf_op jit(solution)/shard_map/dot_general | solution.py:34
  303.9 0.0 reduce-scatter.2.cloned.1.call-update
  304.0 0.2 copy.15
  304.2 20.2 %reduce-scatter.2.cloned.1.call-done = bf16[1024,256]{0,1:T(8,128)(2,1)} async-done(((bf16[2048,256]{0,1:T(8,128)(2,1)}), bf16[1024,256]{0,1:T(8,128)(2,1)}) %reduce-scatter.2.cloned.1.call-update) | async-done | bytes 524304 | tf_op jit(solution)/shard_map/reduce_scatter | solution.py:33
  324.4 0.0 copy-done.2
  324.4 1.3 add_convert_fusion
  325.7 1.0 copy.19
  (2 shorter events, 0.0 us)
Async XLA Ops:
  6.5 172.6 %copy-start = (s32[16]{0:T(128)S(1)}, s32[16]{0:T(128)}, u32[]{:S(2)}) copy-start(s32[16]{0:T(128)} %param.7) | copy-start | bytes 196
  173.3 5.9 %copy-start.1 = (bf16[1024,256]{1,0:T(8,128)(2,1)S(1)}, bf16[1024,256]{1,0:T(8,128)(2,1)}, u32[]{:S(2)}) copy-start(bf16[1024,256]{1,0:T(8,128)(2,1)} %param.5) | copy-start | bytes 1572868
  173.3 63.5 %all-to-all-start.1 = ((bf16[2,2,524288]{2,1,0:T(2,128)(2,1)}), bf16[2,2,524288]{2,1,0:T(2,128)(2,1)}, u32[]{:S(2)}, u32[]{:S(2)}) async-start(bf16[2,2,524288]{2,1,0:T(2,128)(2,1)} %reshape.13), calls=%async_computation.1 | async-start | bytes 8388608 | tf_op jit(solution)/shard_map/all_to_all | solution.py:21
  179.0 78.1 %all-gather.2.cloned.1.call-start = ((), (), s32[]{:S(2)}) async-start(), calls=%async_computation.3 | async-start | bytes 1572864 | tf_op jit(solution)/shard_map/all_gather | solution.py:30
  180.2 119.1 %all-reduce.2.cloned.1.call-start = ((), (), s32[]{:S(2)}) async-start(), calls=%async_computation.4 | async-start | bytes 1048576 | tf_op jit(solution)/shard_map/psum | solution.py:31
  261.8 62.6 %copy-start.2 = (f32[1024]{0:T(1024)S(1)}, f32[1024]{0:T(1024)}, u32[]{:S(2)}) copy-start(f32[1024]{0:T(1024)} %param.6) | copy-start | bytes 12292
  261.8 62.6 %reduce-scatter.2.cloned.1.call-start = ((), (), s32[]{:S(2)}) async-start(), calls=%async_computation.5 | async-start | bytes 1572864 | tf_op jit(solution)/shard_map/reduce_scatter | solution.py:33
Sparse Core Ops, SparseCore 0:
  181.4 32.5 all-gather.1
  261.9 37.3 all-reduce.1
  304.1 20.2 reduce-scatter.1
where the time goes:
time: 334 us; the launch traced here: 333 us
  waiting for transfers between devices  114 us (34%)
  blocking collectives  99.5 us (30%)
  local copies, waits for them, and re-layouts  62.9 us (19%)
  other arithmetic  28.2 us (8%)
  between operations  13.2 us (4%)
  matrix products  9.21 us (3%)
  starting transfers between devices  5.88 us (2%)
    all_to_all x1, blocking collectives, body(): lax.all_to_all(b_built, 'pair', split_axis=1, concat_axis=3, tiled=True)  99.5 us
    all_to_all x1, waiting for transfers between devices, body(): lax.all_to_all(lax.all_to_all(b_built, 'pair', split_axis=1, concat_axis=...  56.5 us
    psum x1, waiting for transfers between devices, body(): coeffs = lax.psum(aux_partial.astype(jnp.bfloat16), 'pair')  37.5 us
    all_to_all x1, local copies, waits for them, and re-layouts, body(): lax.all_to_all(b_built, 'pair', split_axis=1, concat_axis=3, tiled=True)  28.6 us
    unnamed x12, local copies, waits for them, and re-layouts  27.1 us
    unnamed x1, other arithmetic  26 us
    reduce_scatter x1, waiting for transfers between devices, body(): lax.psum_scatter(jnp.dot(part_rows, coeffs, preferred_element_type=jnp.fl...  20.2 us
  transfers between devices with their start and end apart: 4, of which 3 were waited for; matrix products, arithmetic and copies ran while one was open for 6% of the time, Pallas kernels for 0%

commit v1 on v0

v1 whole, which is shorter than its diff:
```python
import jax
import jax.numpy as jnp
from jax import lax
from jax.sharding import PartitionSpec as P

BLK = 128
V_PARTS = 2


def contract_rows(left, right):
    return lax.dot_general(
        left, right, (((0,), (0,)), ((), ())), preferred_element_type=jnp.float32
    )


def exchange_sum(partial, n_aux):
    sent = partial.astype(jnp.bfloat16)
    if n_aux == 1:
        return sent
    if n_aux == 2:
        other = lax.ppermute(sent, "aux", [(0, 1), (1, 0)])
        return (partial + other.astype(jnp.float32)).astype(jnp.bfloat16)
    return lax.psum(sent, "aux")


def body(n_pair, n_aux, b_built, trial, energy_gap, block_live):
    rows, vecs = trial.shape
    blocks = rows // BLK
    me = lax.axis_index("pair")
    own_blocks = lax.dynamic_slice_in_dim(block_live, lax.axis_index("aux") * blocks, blocks, 0)
    own_live = jnp.repeat(own_blocks, BLK)
    masked = trial * own_live.astype(jnp.bfloat16)[:, None]
    factors = b_built[0]

    def factor(pair):
        return lax.dynamic_index_in_dim(factors, pair, 0, keepdims=False)

    up = {k: [(z, z + 1) for z in range(k - 1, n_pair - 1)] for k in range(1, n_pair)}
    down = {k: [(z, z - 1) for z in range(n_pair - k, 0, -1)] for k in range(1, n_pair)}

    width = vecs // V_PARTS
    outs = []
    for part in range(V_PARTS):
        own = masked[:, part * width : (part + 1) * width]
        partial = contract_rows(factor(me), own)
        from_below, from_above = {0: own}, {0: own}
        for k in range(1, n_pair):
            from_below[k] = lax.ppermute(from_below[k - 1], "pair", up[k])
            from_above[k] = lax.ppermute(from_above[k - 1], "pair", down[k])
        for k in range(1, n_pair):
            got = from_below[k] + from_above[n_pair - k]
            partial = partial + contract_rows(factor((me - k) % n_pair), got)
        coeffs = exchange_sum(partial, n_aux)

        def share(pair):
            return jnp.dot(factor(pair), coeffs, preferred_element_type=jnp.float32)

        shares = {k: share((me + k) % n_pair) for k in range(n_pair)}
        going_up = going_down = None
        for k in range(n_pair - 1, 0, -1):
            rise, fall = shares[k], shares[n_pair - k]
            if going_up is not None:
                rise = rise + going_up.astype(jnp.float32)
                fall = fall + going_down.astype(jnp.float32)
            going_up = lax.ppermute(
                rise.astype(jnp.bfloat16), "pair", [(z, z + 1) for z in range(0, n_pair - k)]
            )
            going_down = lax.ppermute(
                fall.astype(jnp.bfloat16), "pair", [(z, z - 1) for z in range(n_pair - 1, k - 1, -1)]
            )
        response = shares[0] + going_up.astype(jnp.float32) + going_down.astype(jnp.float32)
        outs.append(response)
    response = jnp.concatenate(outs, axis=1)
    sigma_out = (
        energy_gap[:, None] * trial.astype(jnp.float32)
        + 2.0 * own_live.astype(jnp.float32)[:, None] * response
    )
    return sigma_out.astype(jnp.bfloat16)


def solution(mesh):
    n_pair, n_aux = mesh.shape["pair"], mesh.shape["aux"]
    return jax.shard_map(
        lambda *args: body(n_pair, n_aux, *args),
        mesh=mesh,
        in_specs=(
            P(("traj", "aux"), None, None, "pair"),
            P(("traj", "pair", "aux"), "root"),
            P(("traj", "pair", "aux")),
            P(("traj", "pair")),
        ),
        out_specs=P(("traj", "pair", "aux"), "root"),
        check_vma=False,
    )
```

time: 334 us -> 107 us (0.32)
  blocking collectives: 99.5 us -> 0 us
  waiting for transfers between devices: 114 us -> 24.6 us
  local copies, waits for them, and re-layouts: 62.9 us -> 1.41 us
  starting transfers between devices: 5.88 us -> 57.1 us
  other arithmetic: 28.2 us -> 4.77 us
  between operations: 13.2 us -> 0.6 us
  matrix products: 9.21 us -> 17.7 us
    all_to_all x1 -> x0, blocking collectives: 99.5 us -> none  [body(): lax.all_to_all(b_built, 'pair', split_axis=1, concat_axis=3, tiled=True)]
    ppermute x0 -> x26, starting transfers between devices: none -> 57.1 us  [the longest x6 29.1 us: body(): lax.ppermute(rise.astype(jnp.bfloat16), 'pair', [(z, z + 1) for z in rang...]
    all_to_all x1 -> x0, waiting for transfers between devices: 56.5 us -> none  [body(): lax.all_to_all(lax.all_to_all(b_built, 'pair', split_axis=1, concat_axis=...]
    psum x1 -> x0, waiting for transfers between devices: 37.5 us -> none  [body(): coeffs = lax.psum(aux_partial.astype(jnp.bfloat16), 'pair')]
    all_to_all x2 -> x0, local copies, waits for them, and re-layouts: 34.8 us -> none  [the longest x1 28.6 us: body(): lax.all_to_all(b_built, 'pair', split_axis=1, concat_axis=3, tiled=True)]
    unnamed x12 -> x9, local copies, waits for them, and re-layouts: 27.1 us -> 0.23 us
    unnamed x1 -> x0, other arithmetic: 26 us -> none
    ppermute x0 -> x26, waiting for transfers between devices: none -> 24.6 us  [the longest x6 11 us: body(): from_above[k] = lax.ppermute(from_above[k - 1], 'pair', down[k])]
  transfers between devices with their start and end apart: 4 -> 26, of which waited for: 3 -> 11; matrix products, arithmetic and copies ran while one was open for 6% -> 18% of each run, Pallas kernels for 0% -> 0%
where the time goes in v1:
time: 107 us; the launch traced here: 106 us
  starting transfers between devices  57.1 us (53%)
  waiting for transfers between devices  24.6 us (23%)
  matrix products  17.7 us (17%)
  other arithmetic  4.77 us (4%)
  local copies, waits for them, and re-layouts  1.41 us (1%)
    ppermute x6, starting transfers between devices, body(): lax.ppermute(rise.astype(jnp.bfloat16), 'pair', [(z, z + 1) for z in rang...  29.1 us
    ppermute x6, starting transfers between devices, body(): from_below[k] = lax.ppermute(from_below[k - 1], 'pair', up[k])  12.8 us
    ppermute x6, waiting for transfers between devices, body(): from_above[k] = lax.ppermute(from_above[k - 1], 'pair', down[k])  11 us
    dot_general x8, matrix products, contract_rows(): lax.dot_general(left, right, (((0,), (0,)), ((), ())), preferred_element_...  8.88 us
    dot_general x8, matrix products, share(): return jnp.dot(factor(pair), coeffs, preferred_element_type=jnp.float32)  8.81 us
    ppermute x6, starting transfers between devices, body(): from_above[k] = lax.ppermute(from_above[k - 1], 'pair', down[k])  7.72 us
    ppermute x6, waiting for transfers between devices, body(): lax.ppermute(fall.astype(jnp.bfloat16), 'pair', [(z, z - 1) for z in rang...  5.91 us
    ppermute x6, starting transfers between devices, body(): lax.ppermute(fall.astype(jnp.bfloat16), 'pair', [(z, z - 1) for z in rang...  5.27 us
  transfers between devices with their start and end apart: 26, of which 11 were waited for; matrix products, arithmetic and copies ran while one was open for 18% of the time, Pallas kernels for 0%

profile of v1, /device:TPU:0, one launch (start us, length us, event | category | flops | bytes accessed | tf_op | source)
XLA Modules:
  0.0 106.1 jit_solution(6797292401023746646)
XLA Ops:
  0.0 0.7 dynamic-slice_convert_fusion
  0.7 0.1 broadcast_bitcast_fusion.1
  0.8 1.2 %broadcast_multiply_fusion = bf16[1024,256]{1,0:T(8,128)(2,1)S(1)} fusion(bf16[1024,256]{1,0:T(8,128)(2,1)} %param.5, bf16[1024]{0:T(1024)(128)(2,1)S(1)} %broadcast_bitcast_fusion.1), kind=kLoop, calls=%fused_computation.69 | loop fusion | flops 262144 | bytes 1050624 | tf_op jit(solution)/shard_map/mul | solution.py:32
  2.1 1.3 %collective-permute-start.14 = (bf16[1024,128]{1,0:T(8,128)(2,1)S(1)}, bf16[1024,128]{1,0:T(8,128)(2,1)S(1)}, u32[]{:S(2)}, u32[]{:S(2)}) collective-permute-start(bf16[1024,128]{1,0:T(8,128)(2,1)S(1)} %get-tuple-element.8), channel_id=1, source_target_pairs={{12,8},{8,4},{4,0},{13,9},{9,5},{5,1},{14,10},{10,6},{6,2},{15,11}... | collective-permute-start | bytes 786440 | tf_op jit(solution)/shard_map/ppermute | solution.py:49
  3.4 5.6 %collective-permute-start.13 = (bf16[1024,128]{1,0:T(8,128)(2,1)S(1)}, bf16[1024,128]{1,0:T(8,128)(2,1)S(1)}, u32[]{:S(2)}, u32[]{:S(2)}) collective-permute-start(bf16[1024,128]{1,0:T(8,128)(2,1)S(1)} %get-tuple-element.8), channel_id=1, source_target_pairs={{0,4},{4,8},{8,12},{1,5},{5,9},{9,13},{2,6},{6,10},{10,14},{3,7},{... | collective-permute-start | bytes 786440 | tf_op jit(solution)/shard_map/ppermute | solution.py:48
  9.0 1.3 %collective-permute-start.1 = (bf16[1024,128]{1,0:T(8,128)(2,1)S(1)}, bf16[1024,128]{1,0:T(8,128)(2,1)S(1)}, u32[]{:S(2)}, u32[]{:S(2)}) collective-permute-start(bf16[1024,128]{1,0:T(8,128)(2,1)S(1)} %get-tuple-element.7), channel_id=1, source_target_pairs={{12,8},{8,4},{4,0},{13,9},{9,5},{5,1},{14,10},{10,6},{6,2},{15,11}... | collective-permute-start | bytes 786440 | tf_op jit(solution)/shard_map/ppermute | solution.py:49
  10.3 4.6 %collective-permute-start = (bf16[1024,128]{1,0:T(8,128)(2,1)S(1)}, bf16[1024,128]{1,0:T(8,128)(2,1)S(1)}, u32[]{:S(2)}, u32[]{:S(2)}) collective-permute-start(bf16[1024,128]{1,0:T(8,128)(2,1)S(1)} %get-tuple-element.7), channel_id=1, source_target_pairs={{0,4},{4,8},{8,12},{1,5},{5,9},{9,13},{2,6},{6,10},{10,14},{3,7},{... | collective-permute-start | bytes 786440 | tf_op jit(solution)/shard_map/ppermute | solution.py:48
  14.9 1.3 %collective-permute-start.15 = (bf16[1024,128]{1,0:T(8,128)(2,1)S(1)}, bf16[1024,128]{1,0:T(8,128)(2,1)S(1)}, u32[]{:S(2)}, u32[]{:S(2)}) collective-permute-start(bf16[1024,128]{1,0:T(8,128)(2,1)S(1)} %collective-permute-done.14), channel_id=1, source_target_pairs={{8,4},{4,0},{9,5},{5,1},{10,6},{6,2},{11,7},{7,3},{24,20},{20,16},... | collective-permute-start | bytes 786440 | tf_op jit(solution)/shard_map/ppermute | solution.py:49
  16.2 0.7 collective-permute-start.17
  16.9 2.6 %collective-permute-done.1 = bf16[1024,128]{1,0:T(8,128)(2,1)S(1)} collective-permute-done((bf16[1024,128]{1,0:T(8,128)(2,1)S(1)}, bf16[1024,128]{1,0:T(8,128)(2,1)S(1)}, u32[]{:S(2)}, u32[]{:S(2)}) %collective-permute-start.1) | collective-permute-done | bytes 262176 | tf_op jit(solution)/shard_map/ppermute | solution.py:49
  19.5 1.3 %collective-permute-start.2 = (bf16[1024,128]{1,0:T(8,128)(2,1)S(1)}, bf16[1024,128]{1,0:T(8,128)(2,1)S(1)}, u32[]{:S(2)}, u32[]{:S(2)}) collective-permute-start(bf16[1024,128]{1,0:T(8,128)(2,1)S(1)} %collective-permute-done.1), channel_id=1, source_target_pairs={{8,4},{4,0},{9,5},{5,1},{10,6},{6,2},{11,7},{7,3},{24,20},{20,16},... | collective-permute-start | bytes 786440 | tf_op jit(solution)/shard_map/ppermute | solution.py:49
  20.8 0.7 collective-permute-start.4
  21.5 3.9 %collective-permute-done.15 = bf16[1024,128]{1,0:T(8,128)(2,1)S(1)} collective-permute-done((bf16[1024,128]{1,0:T(8,128)(2,1)S(1)}, bf16[1024,128]{1,0:T(8,128)(2,1)S(1)}, u32[]{:S(2)}, u32[]{:S(2)}) %collective-permute-start.15) | collective-permute-done | bytes 262176 | tf_op jit(solution)/shard_map/ppermute | solution.py:49
  25.4 1.3 %collective-permute-start.16 = (bf16[1024,128]{1,0:T(8,128)(2,1)S(1)}, bf16[1024,128]{1,0:T(8,128)(2,1)S(1)}, u32[]{:S(2)}, u32[]{:S(2)}) collective-permute-start(bf16[1024,128]{1,0:T(8,128)(2,1)S(1)} %collective-permute-done.15), channel_id=1, source_target_pairs={{4,0},{5,1},{6,2},{7,3},{20,16},{21,17},{22,18},{23,19}} | collective-permute-start | bytes 786440 | tf_op jit(solution)/shard_map/ppermute | solution.py:49
  26.7 1.7 %fusion.22 = f32[512,128]{1,0:T(8,128)S(1)} fusion(bf16[1,4,1024,512]{3,2,1,0:T(8,128)(2,1)} %param.4, s32[]{:T(128)S(6)} %select_n.84, bf16[1024,256]{1,0:T(8,128)(2,1)S(1)} %broadcast_multiply_fusion), kind=kOutput, calls=%fused_computation.31 | convolution fusion | flops 134217728 | bytes 1572868 | tf_op jit(solution)/shard_map/dot_general | solution.py:11
  28.5 1.8 %fusion.24 = f32[512,128]{1,0:T(8,128)S(1)} fusion(bf16[1,4,1024,512]{3,2,1,0:T(8,128)(2,1)} %param.4, s32[]{:T(128)S(6)} %select_n.84, bf16[1024,256]{1,0:T(8,128)(2,1)S(1)} %broadcast_multiply_fusion), kind=kOutput, calls=%fused_computation.33 | convolution fusion | flops 134217728 | bytes 1572868 | tf_op jit(solution)/shard_map/dot_general | solution.py:11
  30.3 0.7 collective-permute-start.18
  31.0 0.8 collective-permute-done.2
  31.9 1.3 %collective-permute-start.3 = (bf16[1024,128]{1,0:T(8,128)(2,1)S(1)}, bf16[1024,128]{1,0:T(8,128)(2,1)S(1)}, u32[]{:S(2)}, u32[]{:S(2)}) collective-permute-start(bf16[1024,128]{1,0:T(8,128)(2,1)S(1)} %collective-permute-done.2), channel_id=1, source_target_pairs={{4,0},{5,1},{6,2},{7,3},{20,16},{21,17},{22,18},{23,19}} | collective-permute-start | bytes 786440 | tf_op jit(solution)/shard_map/ppermute | solution.py:49
  33.2 0.7 collective-permute-start.5
  33.9 3.6 %collective-permute-done.16 = bf16[1024,128]{1,0:T(8,128)(2,1)S(1)} collective-permute-done((bf16[1024,128]{1,0:T(8,128)(2,1)S(1)}, bf16[1024,128]{1,0:T(8,128)(2,1)S(1)}, u32[]{:S(2)}, u32[]{:S(2)}) %collective-permute-start.16) | collective-permute-done | bytes 262176 | tf_op jit(solution)/shard_map/ppermute | solution.py:49
  37.5 1.7 %convolution_add_fusion.4 = f32[512,128]{1,0:T(8,128)S(1)} fusion(f32[512,128]{1,0:T(8,128)S(1)} %fusion.22, bf16[1,4,1024,512]{3,2,1,0:T(8,128)(2,1)} %param.4, s32[]{:T(128)S(6)} %select_n.86, bf16[1024,128]{1,0:T(8,128)(2,1)S(1)} %collective-permute-done.13, bf16[1024,128]{1,0:T(8,128)(2,1)S(1)} %collective-permute-done.16), kind=kOutput, calls=%fused_computation.6 | convolution fusion | flops 134414336 | bytes 2097156 | tf_op jit(solution)/shard_map/dot_general | solution.py:11
  39.2 1.7 %convolution_add_fusion.3 = f32[512,128]{1,0:T(8,128)S(1)} fusion(f32[512,128]{1,0:T(8,128)S(1)} %convolution_add_fusion.4, bf16[1,4,1024,512]{3,2,1,0:T(8,128)(2,1)} %param.4, s32[]{:T(128)S(6)} %select_n.88, bf16[1024,128]{1,0:T(8,128)(2,1)S(1)} %collective-permute-done.17, bf16[1024,128]{1,0:T(8,128)(2,1)S(1)} %collective-permute-done.15), kind=kOutput, calls=%fused_computation.5 | convolution fusion | flops 134414336 | bytes 2097156 | tf_op jit(solution)/shard_map/dot_general | solution.py:11
  40.9 0.5 fusion.70
  41.4 1.6 %collective-permute-start.19 = (bf16[512,128]{1,0:T(8,128)(2,1)S(1)}, bf16[512,128]{1,0:T(8,128)(2,1)S(1)}, u32[]{:S(2)}, u32[]{:S(2)}) collective-permute-start(bf16[512,128]{1,0:T(8,128)(2,1)S(1)} %get-tuple-element.13), channel_id=1, source_target_pairs={{0,2},{2,0},{1,3},{3,1},{4,6},{6,4},{5,7},{7,5},{8,10},{10,8},{9,1... | collective-permute-start | bytes 393224 | tf_op jit(solution)/shard_map/ppermute | solution.py:21
  43.0 0.5 convolution_add_fusion.7
  43.5 0.5 convolution_add_fusion.6
  44.0 0.5 fusion.69
  44.4 0.6 collective-permute-start.6
  45.0 1.8 %collective-permute-done.19 = bf16[512,128]{1,0:T(8,128)(2,1)S(1)} collective-permute-done((bf16[512,128]{1,0:T(8,128)(2,1)S(1)}, bf16[512,128]{1,0:T(8,128)(2,1)S(1)}, u32[]{:S(2)}, u32[]{:S(2)}) %collective-permute-start.19) | collective-permute-done | bytes 131104 | tf_op jit(solution)/shard_map/ppermute | solution.py:21
  46.9 0.5 fusion.71
  47.4 1.5 %collective-permute-start.20 = (bf16[1024,128]{0,1:T(8,128)(2,1)S(1)}, bf16[1024,128]{0,1:T(8,128)(2,1)S(1)}, u32[]{:S(2)}, u32[]{:S(2)}) collective-permute-start(bf16[1024,128]{0,1:T(8,128)(2,1)S(1)} %get-tuple-element.15), channel_id=1, source_target_pairs={{0,4},{1,5},{2,6},{3,7},{16,20},{17,21},{18,22},{19,23}} | collective-permute-start | bytes 786440 | tf_op jit(solution)/shard_map/ppermute | solution.py:65
  48.8 0.6 collective-permute-done.6
  49.5 0.5 fusion.72
  50.0 0.5 fusion.8
  50.5 1.5 %collective-permute-start.7 = (bf16[1024,128]{0,1:T(8,128)(2,1)S(1)}, bf16[1024,128]{0,1:T(8,128)(2,1)S(1)}, u32[]{:S(2)}, u32[]{:S(2)}) collective-permute-start(bf16[1024,128]{0,1:T(8,128)(2,1)S(1)} %get-tuple-element.17), channel_id=1, source_target_pairs={{0,4},{1,5},{2,6},{3,7},{16,20},{17,21},{18,22},{19,23}} | collective-permute-start | bytes 786440 | tf_op jit(solution)/shard_map/ppermute | solution.py:65
  52.0 0.5 fusion.10
  52.5 3.1 %collective-permute-done.20 = bf16[1024,128]{0,1:T(8,128)(2,1)S(1)} collective-permute-done((bf16[1024,128]{0,1:T(8,128)(2,1)S(1)}, bf16[1024,128]{0,1:T(8,128)(2,1)S(1)}, u32[]{:S(2)}, u32[]{:S(2)}) %collective-permute-start.20) | collective-permute-done | bytes 262176 | tf_op jit(solution)/shard_map/ppermute | solution.py:65
  55.6 4.4 %collective-permute-start.21 = (bf16[1024,128]{0,1:T(8,128)(2,1)S(1)}, bf16[1024,128]{0,1:T(8,128)(2,1)S(1)}, u32[]{:S(2)}, u32[]{:S(2)}) collective-permute-start(bf16[1024,128]{0,1:T(8,128)(2,1)S(1)} %add_convert_fusion.3), channel_id=1, source_target_pairs={{0,4},{4,8},{1,5},{5,9},{2,6},{6,10},{3,7},{7,11},{16,20},{20,24},... | collective-permute-start | bytes 786440 | tf_op jit(solution)/shard_map/ppermute | solution.py:65
  60.0 1.0 collective-permute-done.7
  61.0 0.8 add_convert_fusion.7
  61.8 5.2 %collective-permute-start.8 = (bf16[1024,128]{0,1:T(8,128)(2,1)}, bf16[1024,128]{0,1:T(8,128)(2,1)}, u32[]{:S(2)}, u32[]{:S(2)}) collective-permute-start(bf16[1024,128]{0,1:T(8,128)(2,1)} %add_convert_fusion.7), channel_id=1, source_target_pairs={{0,4},{4,8},{1,5},{5,9},{2,6},{6,10},{3,7},{7,11},{16,20},{20,24},... | collective-permute-start | bytes 786440 | tf_op jit(solution)/shard_map/ppermute | solution.py:65
  67.0 1.7 %add_convert_fusion.2 = (bf16[1024,128]{0,1:T(8,128)(2,1)S(1)}, bf16[1024,128]{0,1:T(8,128)(2,1)S(1)}) fusion(bf16[1024,128]{0,1:T(8,128)(2,1)S(1)} %collective-permute-done.21, bf16[512,128]{1,0:T(8,128)(2,1)S(1)} %add_convert_fusion.8, bf16[1,4,1024,512]{3,2,1,0:T(8,128)(2,1)} %param.4, s32[]{:T(128)S(6)} %select_n.92), kind=kOutput, calls=%fused_computation.55 | convolution fusion | flops 134742016 | bytes 1966084 | tf_op jit(solution)/shard_map/dot_general | solution.py:56
  68.7 0.7 collective-permute-start.23
  69.4 1.1 %collective-permute-done.8 = bf16[1024,128]{0,1:T(8,128)(2,1)} collective-permute-done((bf16[1024,128]{0,1:T(8,128)(2,1)}, bf16[1024,128]{0,1:T(8,128)(2,1)}, u32[]{:S(2)}, u32[]{:S(2)}) %collective-permute-start.8) | collective-permute-done | bytes 262176 | tf_op jit(solution)/shard_map/ppermute | solution.py:65
  70.5 1.7 %add_convert_fusion.6 = (bf16[1024,128]{0,1:T(8,128)(2,1)S(1)}, bf16[1024,128]{0,1:T(8,128)(2,1)S(1)}) fusion(bf16[1024,128]{0,1:T(8,128)(2,1)} %collective-permute-done.8, bf16[512,128]{1,0:T(8,128)(2,1)S(1)} %add_convert_fusion.9, bf16[1,4,1024,512]{3,2,1,0:T(8,128)(2,1)} %param.4, s32[]{:T(128)S(6)} %select_n.92), kind=kOutput, calls=%fused_computation.59 | convolution fusion | flops 134742016 | bytes 1966084 | tf_op jit(solution)/shard_map/dot_general | solution.py:56
  72.2 0.7 collective-permute-start.10
  73.0 0.7 collective-permute-start.24
  73.8 0.7 collective-permute-start.11
  74.5 0.1 convert_multiply_fusion
  74.5 5.6 %collective-permute-start.22 = (bf16[1024,128]{0,1:T(8,128)(2,1)S(1)}, bf16[1024,128]{0,1:T(8,128)(2,1)S(1)}, u32[]{:S(2)}, u32[]{:S(2)}) collective-permute-start(bf16[1024,128]{0,1:T(8,128)(2,1)S(1)} %get-tuple-element.9), channel_id=1, source_target_pairs={{0,4},{4,8},{8,12},{1,5},{5,9},{9,13},{2,6},{6,10},{10,14},{3,7},{... | collective-permute-start | bytes 786440 | tf_op jit(solution)/shard_map/ppermute | solution.py:65
  80.2 10.9 %collective-permute-start.9 = (bf16[1024,128]{0,1:T(8,128)(2,1)S(1)}, bf16[1024,128]{0,1:T(8,128)(2,1)S(1)}, u32[]{:S(2)}, u32[]{:S(2)}) collective-permute-start(bf16[1024,128]{0,1:T(8,128)(2,1)S(1)} %get-tuple-element.5), channel_id=1, source_target_pairs={{0,4},{4,8},{8,12},{1,5},{5,9},{9,13},{2,6},{6,10},{10,14},{3,7},{... | collective-permute-start | bytes 786440 | tf_op jit(solution)/shard_map/ppermute | solution.py:65
  91.1 0.8 add_convert_fusion
  91.9 1.3 %collective-permute-start.25 = (bf16[1024,128]{0,1:T(8,128)(2,1)}, bf16[1024,128]{0,1:T(8,128)(2,1)S(1)}, u32[]{:S(2)}, u32[]{:S(2)}) collective-permute-start(bf16[1024,128]{0,1:T(8,128)(2,1)} %add_convert_fusion), channel_id=1, source_target_pairs={{12,8},{8,4},{4,0},{13,9},{9,5},{5,1},{14,10},{10,6},{6,2},{15,11}... | collective-permute-start | bytes 786440 | tf_op jit(solution)/shard_map/ppermute | solution.py:68
  93.2 0.8 add_convert_fusion.4
  94.0 1.3 %collective-permute-start.12 = (bf16[1024,128]{0,1:T(8,128)(2,1)}, bf16[1024,128]{0,1:T(8,128)(2,1)S(1)}, u32[]{:S(2)}, u32[]{:S(2)}) collective-permute-start(bf16[1024,128]{0,1:T(8,128)(2,1)} %add_convert_fusion.4), channel_id=1, source_target_pairs={{12,8},{8,4},{4,0},{13,9},{9,5},{5,1},{14,10},{10,6},{6,2},{15,11}... | collective-permute-start | bytes 786440 | tf_op jit(solution)/shard_map/ppermute | solution.py:68
  95.2 0.1 broadcast_bitcast_fusion
  95.3 0.2 copy.5
  95.6 4.8 %collective-permute-done.25 = bf16[1024,128]{0,1:T(8,128)(2,1)S(1)} collective-permute-done((bf16[1024,128]{0,1:T(8,128)(2,1)}, bf16[1024,128]{0,1:T(8,128)(2,1)S(1)}, u32[]{:S(2)}, u32[]{:S(2)}) %collective-permute-start.25) | collective-permute-done | bytes 262176 | tf_op jit(solution)/shard_map/ppermute | solution.py:68
  100.4 1.7 %fusion.1 = f32[1024,128]{0,1:T(8,128)S(1)} fusion(bf16[512,128]{1,0:T(8,128)(2,1)S(1)} %add_convert_fusion.8, bf16[1,4,1024,512]{3,2,1,0:T(8,128)(2,1)} %param.4, s32[]{:T(128)S(6)} %select_n.83, bf16[1024,128]{0,1:T(8,128)(2,1)S(1)} %collective-permute-done.25, bf16[1024,128]{0,1:T(8,128)(2,1)S(1)} %collective-permute-done.22), kind=kOutput, calls=%fused_computation.3 | convolution fusion | flops 134742016 | bytes 2228228 | tf_op jit(solution)/shard_map/dot_general | solution.py:56
  102.1 1.1 %collective-permute-done.12 = bf16[1024,128]{0,1:T(8,128)(2,1)S(1)} collective-permute-done((bf16[1024,128]{0,1:T(8,128)(2,1)}, bf16[1024,128]{0,1:T(8,128)(2,1)S(1)}, u32[]{:S(2)}, u32[]{:S(2)}) %collective-permute-start.12) | collective-permute-done | bytes 262176 | tf_op jit(solution)/shard_map/ppermute | solution.py:68
  103.2 1.7 %fusion = f32[1024,128]{0,1:T(8,128)S(1)} fusion(bf16[512,128]{1,0:T(8,128)(2,1)S(1)} %add_convert_fusion.9, bf16[1,4,1024,512]{3,2,1,0:T(8,128)(2,1)} %param.4, s32[]{:T(128)S(6)} %select_n.83, bf16[1024,128]{0,1:T(8,128)(2,1)S(1)} %collective-permute-done.12, bf16[1024,128]{0,1:T(8,128)(2,1)S(1)} %collective-permute-done.9), kind=kOutput, calls=%fused_computation.2 | convolution fusion | flops 134742016 | bytes 2228228 | tf_op jit(solution)/shard_map/dot_general | solution.py:56
  104.9 0.2 fusion.3
  105.1 1.0 copy.18
  (29 shorter events, 0.3 us)
Async XLA Ops:
  2.1 12.8 %collective-permute-start.14 = (bf16[1024,128]{1,0:T(8,128)(2,1)S(1)}, bf16[1024,128]{1,0:T(8,128)(2,1)S(1)}, u32[]{:S(2)}, u32[]{:S(2)}) collective-permute-start(bf16[1024,128]{1,0:T(8,128)(2,1)S(1)} %get-tuple-element.8), channel_id=1, source_target_pairs={{12,8},{8,4},{4,0},{13,9},{9,5},{5,1},{14,10},{10,6},{6,2},{15,11}... | collective-permute-start | bytes 786440 | tf_op jit(solution)/shard_map/ppermute | solution.py:49
  3.4 12.8 %collective-permute-start.13 = (bf16[1024,128]{1,0:T(8,128)(2,1)S(1)}, bf16[1024,128]{1,0:T(8,128)(2,1)S(1)}, u32[]{:S(2)}, u32[]{:S(2)}) collective-permute-start(bf16[1024,128]{1,0:T(8,128)(2,1)S(1)} %get-tuple-element.8), channel_id=1, source_target_pairs={{0,4},{4,8},{8,12},{1,5},{5,9},{9,13},{2,6},{6,10},{10,14},{3,7},{... | collective-permute-start | bytes 786440 | tf_op jit(solution)/shard_map/ppermute | solution.py:48
  9.0 10.5 %collective-permute-start.1 = (bf16[1024,128]{1,0:T(8,128)(2,1)S(1)}, bf16[1024,128]{1,0:T(8,128)(2,1)S(1)}, u32[]{:S(2)}, u32[]{:S(2)}) collective-permute-start(bf16[1024,128]{1,0:T(8,128)(2,1)S(1)} %get-tuple-element.7), channel_id=1, source_target_pairs={{12,8},{8,4},{4,0},{13,9},{9,5},{5,1},{14,10},{10,6},{6,2},{15,11}... | collective-permute-start | bytes 786440 | tf_op jit(solution)/shard_map/ppermute | solution.py:49
  10.3 10.5 %collective-permute-start = (bf16[1024,128]{1,0:T(8,128)(2,1)S(1)}, bf16[1024,128]{1,0:T(8,128)(2,1)S(1)}, u32[]{:S(2)}, u32[]{:S(2)}) collective-permute-start(bf16[1024,128]{1,0:T(8,128)(2,1)S(1)} %get-tuple-element.7), channel_id=1, source_target_pairs={{0,4},{4,8},{8,12},{1,5},{5,9},{9,13},{2,6},{6,10},{10,14},{3,7},{... | collective-permute-start | bytes 786440 | tf_op jit(solution)/shard_map/ppermute | solution.py:48
  14.9 10.5 %collective-permute-start.15 = (bf16[1024,128]{1,0:T(8,128)(2,1)S(1)}, bf16[1024,128]{1,0:T(8,128)(2,1)S(1)}, u32[]{:S(2)}, u32[]{:S(2)}) collective-permute-start(bf16[1024,128]{1,0:T(8,128)(2,1)S(1)} %collective-permute-done.14), channel_id=1, source_target_pairs={{8,4},{4,0},{9,5},{5,1},{10,6},{6,2},{11,7},{7,3},{24,20},{20,16},... | collective-permute-start | bytes 786440 | tf_op jit(solution)/shard_map/ppermute | solution.py:49
  16.2 14.2 %collective-permute-start.17 = (bf16[1024,128]{1,0:T(8,128)(2,1)S(1)}, bf16[1024,128]{1,0:T(8,128)(2,1)S(1)}, u32[]{:S(2)}, u32[]{:S(2)}) collective-permute-start(bf16[1024,128]{1,0:T(8,128)(2,1)S(1)} %collective-permute-done.13), channel_id=1, source_target_pairs={{4,8},{8,12},{5,9},{9,13},{6,10},{10,14},{7,11},{11,15},{20,24},{2... | collective-permute-start | bytes 786440 | tf_op jit(solution)/shard_map/ppermute | solution.py:48
  19.5 12.4 %collective-permute-start.2 = (bf16[1024,128]{1,0:T(8,128)(2,1)S(1)}, bf16[1024,128]{1,0:T(8,128)(2,1)S(1)}, u32[]{:S(2)}, u32[]{:S(2)}) collective-permute-start(bf16[1024,128]{1,0:T(8,128)(2,1)S(1)} %collective-permute-done.1), channel_id=1, source_target_pairs={{8,4},{4,0},{9,5},{5,1},{10,6},{6,2},{11,7},{7,3},{24,20},{20,16},... | collective-permute-start | bytes 786440 | tf_op jit(solution)/shard_map/ppermute | solution.py:49
  20.8 12.4 %collective-permute-start.4 = (bf16[1024,128]{1,0:T(8,128)(2,1)S(1)}, bf16[1024,128]{1,0:T(8,128)(2,1)S(1)}, u32[]{:S(2)}, u32[]{:S(2)}) collective-permute-start(bf16[1024,128]{1,0:T(8,128)(2,1)S(1)} %collective-permute-done), channel_id=1, source_target_pairs={{4,8},{8,12},{5,9},{9,13},{6,10},{10,14},{7,11},{11,15},{20,24},{2... | collective-permute-start | bytes 786440 | tf_op jit(solution)/shard_map/ppermute | solution.py:48
  25.4 12.1 %collective-permute-start.16 = (bf16[1024,128]{1,0:T(8,128)(2,1)S(1)}, bf16[1024,128]{1,0:T(8,128)(2,1)S(1)}, u32[]{:S(2)}, u32[]{:S(2)}) collective-permute-start(bf16[1024,128]{1,0:T(8,128)(2,1)S(1)} %collective-permute-done.15), channel_id=1, source_target_pairs={{4,0},{5,1},{6,2},{7,3},{20,16},{21,17},{22,18},{23,19}} | collective-permute-start | bytes 786440 | tf_op jit(solution)/shard_map/ppermute | solution.py:49
  28.5 12.4 %copy-start = (bf16[1,4,1024,512]{3,2,1,0:T(8,128)(2,1)S(1)}, bf16[1,4,1024,512]{3,2,1,0:T(8,128)(2,1)}, u32[]{:S(2)}) copy-start(bf16[1,4,1024,512]{3,2,1,0:T(8,128)(2,1)} %param.4) | copy-start | bytes 12582916
  30.3 10.6 %collective-permute-start.18 = (bf16[1024,128]{1,0:T(8,128)(2,1)S(1)}, bf16[1024,128]{1,0:T(8,128)(2,1)S(1)}, u32[]{:S(2)}, u32[]{:S(2)}) collective-permute-start(bf16[1024,128]{1,0:T(8,128)(2,1)S(1)} %collective-permute-done.17), channel_id=1, source_target_pairs={{8,12},{9,13},{10,14},{11,15},{24,28},{25,29},{26,30},{27,31}} | collective-permute-start | bytes 786440 | tf_op jit(solution)/shard_map/ppermute | solution.py:48
  31.9 11.1 %collective-permute-start.3 = (bf16[1024,128]{1,0:T(8,128)(2,1)S(1)}, bf16[1024,128]{1,0:T(8,128)(2,1)S(1)}, u32[]{:S(2)}, u32[]{:S(2)}) collective-permute-start(bf16[1024,128]{1,0:T(8,128)(2,1)S(1)} %collective-permute-done.2), channel_id=1, source_target_pairs={{4,0},{5,1},{6,2},{7,3},{20,16},{21,17},{22,18},{23,19}} | collective-permute-start | bytes 786440 | tf_op jit(solution)/shard_map/ppermute | solution.py:49
  33.2 10.8 %collective-permute-start.5 = (bf16[1024,128]{1,0:T(8,128)(2,1)S(1)}, bf16[1024,128]{1,0:T(8,128)(2,1)S(1)}, u32[]{:S(2)}, u32[]{:S(2)}) collective-permute-start(bf16[1024,128]{1,0:T(8,128)(2,1)S(1)} %collective-permute-done.4), channel_id=1, source_target_pairs={{8,12},{9,13},{10,14},{11,15},{24,28},{25,29},{26,30},{27,31}} | collective-permute-start | bytes 786440 | tf_op jit(solution)/shard_map/ppermute | solution.py:48
  41.4 5.4 %collective-permute-start.19 = (bf16[512,128]{1,0:T(8,128)(2,1)S(1)}, bf16[512,128]{1,0:T(8,128)(2,1)S(1)}, u32[]{:S(2)}, u32[]{:S(2)}) collective-permute-start(bf16[512,128]{1,0:T(8,128)(2,1)S(1)} %get-tuple-element.13), channel_id=1, source_target_pairs={{0,2},{2,0},{1,3},{3,1},{4,6},{6,4},{5,7},{7,5},{8,10},{10,8},{9,1... | collective-permute-start | bytes 393224 | tf_op jit(solution)/shard_map/ppermute | solution.py:21
  44.4 5.0 %collective-permute-start.6 = (bf16[512,128]{1,0:T(8,128)(2,1)S(1)}, bf16[512,128]{1,0:T(8,128)(2,1)S(1)}, u32[]{:S(2)}, u32[]{:S(2)}) collective-permute-start(bf16[512,128]{1,0:T(8,128)(2,1)S(1)} %get-tuple-element.11), channel_id=1, source_target_pairs={{0,2},{2,0},{1,3},{3,1},{4,6},{6,4},{5,7},{7,5},{8,10},{10,8},{9,1... | collective-permute-start | bytes 393224 | tf_op jit(solution)/shard_map/ppermute | solution.py:21
  47.4 8.2 %collective-permute-start.20 = (bf16[1024,128]{0,1:T(8,128)(2,1)S(1)}, bf16[1024,128]{0,1:T(8,128)(2,1)S(1)}, u32[]{:S(2)}, u32[]{:S(2)}) collective-permute-start(bf16[1024,128]{0,1:T(8,128)(2,1)S(1)} %get-tuple-element.15), channel_id=1, source_target_pairs={{0,4},{1,5},{2,6},{3,7},{16,20},{17,21},{18,22},{19,23}} | collective-permute-start | bytes 786440 | tf_op jit(solution)/shard_map/ppermute | solution.py:65
  50.5 10.5 %collective-permute-start.7 = (bf16[1024,128]{0,1:T(8,128)(2,1)S(1)}, bf16[1024,128]{0,1:T(8,128)(2,1)S(1)}, u32[]{:S(2)}, u32[]{:S(2)}) collective-permute-start(bf16[1024,128]{0,1:T(8,128)(2,1)S(1)} %get-tuple-element.17), channel_id=1, source_target_pairs={{0,4},{1,5},{2,6},{3,7},{16,20},{17,21},{18,22},{19,23}} | collective-permute-start | bytes 786440 | tf_op jit(solution)/shard_map/ppermute | solution.py:65
  52.5 22.0 %copy-start.3 = (s32[16]{0:T(128)S(1)}, s32[16]{0:T(128)}, u32[]{:S(2)}) copy-start(s32[16]{0:T(128)} %param.7) | copy-start | bytes 196
  55.6 11.4 %collective-permute-start.21 = (bf16[1024,128]{0,1:T(8,128)(2,1)S(1)}, bf16[1024,128]{0,1:T(8,128)(2,1)S(1)}, u32[]{:S(2)}, u32[]{:S(2)}) collective-permute-start(bf16[1024,128]{0,1:T(8,128)(2,1)S(1)} %add_convert_fusion.3), channel_id=1, source_target_pairs={{0,4},{4,8},{1,5},{5,9},{2,6},{6,10},{3,7},{7,11},{16,20},{20,24},... | collective-permute-start | bytes 786440 | tf_op jit(solution)/shard_map/ppermute | solution.py:65
  61.8 33.6 %copy-start.1 = (bf16[1024,256]{1,0:T(8,128)(2,1)S(1)}, bf16[1024,256]{1,0:T(8,128)(2,1)}, u32[]{:S(2)}) copy-start(bf16[1024,256]{1,0:T(8,128)(2,1)} %param.5) | copy-start | bytes 1572868
  61.8 8.7 %collective-permute-start.8 = (bf16[1024,128]{0,1:T(8,128)(2,1)}, bf16[1024,128]{0,1:T(8,128)(2,1)}, u32[]{:S(2)}, u32[]{:S(2)}) collective-permute-start(bf16[1024,128]{0,1:T(8,128)(2,1)} %add_convert_fusion.7), channel_id=1, source_target_pairs={{0,4},{4,8},{1,5},{5,9},{2,6},{6,10},{3,7},{7,11},{16,20},{20,24},... | collective-permute-start | bytes 786440 | tf_op jit(solution)/shard_map/ppermute | solution.py:65
  68.7 4.2 %collective-permute-start.23 = (bf16[1024,128]{0,1:T(8,128)(2,1)S(1)}, bf16[1024,128]{0,1:T(8,128)(2,1)S(1)}, u32[]{:S(2)}, u32[]{:S(2)}) collective-permute-start(bf16[1024,128]{0,1:T(8,128)(2,1)S(1)} %get-tuple-element.10), channel_id=1, source_target_pairs={{12,8},{13,9},{14,10},{15,11},{28,24},{29,25},{30,26},{31,27}} | collective-permute-start | bytes 786440 | tf_op jit(solution)/shard_map/ppermute | solution.py:68
  72.2 1.5 %collective-permute-start.10 = (bf16[1024,128]{0,1:T(8,128)(2,1)S(1)}, bf16[1024,128]{0,1:T(8,128)(2,1)S(1)}, u32[]{:S(2)}, u32[]{:S(2)}) collective-permute-start(bf16[1024,128]{0,1:T(8,128)(2,1)S(1)} %get-tuple-element.6), channel_id=1, source_target_pairs={{12,8},{13,9},{14,10},{15,11},{28,24},{29,25},{30,26},{31,27}} | collective-permute-start | bytes 786440 | tf_op jit(solution)/shard_map/ppermute | solution.py:68
  73.0 31.9 %copy-start.2 = (f32[1024]{0:T(1024)S(1)}, f32[1024]{0:T(1024)}, u32[]{:S(2)}) copy-start(f32[1024]{0:T(1024)} %param.6) | copy-start | bytes 12292
  73.0 18.1 %collective-permute-start.24 = (bf16[1024,128]{0,1:T(8,128)(2,1)S(1)}, bf16[1024,128]{0,1:T(8,128)(2,1)S(1)}, u32[]{:S(2)}, u32[]{:S(2)}) collective-permute-start(bf16[1024,128]{0,1:T(8,128)(2,1)S(1)} %add_convert_fusion.1), channel_id=1, source_target_pairs={{12,8},{8,4},{13,9},{9,5},{14,10},{10,6},{15,11},{11,7},{28,24},{2... | collective-permute-start | bytes 786440 | tf_op jit(solution)/shard_map/ppermute | solution.py:68
  73.8 19.4 %collective-permute-start.11 = (bf16[1024,128]{0,1:T(8,128)(2,1)S(1)}, bf16[1024,128]{0,1:T(8,128)(2,1)S(1)}, u32[]{:S(2)}, u32[]{:S(2)}) collective-permute-start(bf16[1024,128]{0,1:T(8,128)(2,1)S(1)} %add_convert_fusion.5), channel_id=1, source_target_pairs={{12,8},{8,4},{13,9},{9,5},{14,10},{10,6},{15,11},{11,7},{28,24},{2... | collective-permute-start | bytes 786440 | tf_op jit(solution)/shard_map/ppermute | solution.py:68
  74.5 21.0 %collective-permute-start.22 = (bf16[1024,128]{0,1:T(8,128)(2,1)S(1)}, bf16[1024,128]{0,1:T(8,128)(2,1)S(1)}, u32[]{:S(2)}, u32[]{:S(2)}) collective-permute-start(bf16[1024,128]{0,1:T(8,128)(2,1)S(1)} %get-tuple-element.9), channel_id=1, source_target_pairs={{0,4},{4,8},{8,12},{1,5},{5,9},{9,13},{2,6},{6,10},{10,14},{3,7},{... | collective-permute-start | bytes 786440 | tf_op jit(solution)/shard_map/ppermute | solution.py:65
  80.2 21.9 %collective-permute-start.9 = (bf16[1024,128]{0,1:T(8,128)(2,1)S(1)}, bf16[1024,128]{0,1:T(8,128)(2,1)S(1)}, u32[]{:S(2)}, u32[]{:S(2)}) collective-permute-start(bf16[1024,128]{0,1:T(8,128)(2,1)S(1)} %get-tuple-element.5), channel_id=1, source_target_pairs={{0,4},{4,8},{8,12},{1,5},{5,9},{9,13},{2,6},{6,10},{10,14},{3,7},{... | collective-permute-start | bytes 786440 | tf_op jit(solution)/shard_map/ppermute | solution.py:65
  91.9 8.5 %collective-permute-start.25 = (bf16[1024,128]{0,1:T(8,128)(2,1)}, bf16[1024,128]{0,1:T(8,128)(2,1)S(1)}, u32[]{:S(2)}, u32[]{:S(2)}) collective-permute-start(bf16[1024,128]{0,1:T(8,128)(2,1)} %add_convert_fusion), channel_id=1, source_target_pairs={{12,8},{8,4},{4,0},{13,9},{9,5},{5,1},{14,10},{10,6},{6,2},{15,11}... | collective-permute-start | bytes 786440 | tf_op jit(solution)/shard_map/ppermute | solution.py:68
  94.0 9.2 %collective-permute-start.12 = (bf16[1024,128]{0,1:T(8,128)(2,1)}, bf16[1024,128]{0,1:T(8,128)(2,1)S(1)}, u32[]{:S(2)}, u32[]{:S(2)}) collective-permute-start(bf16[1024,128]{0,1:T(8,128)(2,1)} %add_convert_fusion.4), channel_id=1, source_target_pairs={{12,8},{8,4},{4,0},{13,9},{9,5},{5,1},{14,10},{10,6},{6,2},{15,11}... | collective-permute-start | bytes 786440 | tf_op jit(solution)/shard_map/ppermute | solution.py:68

commit v2 on v0

v2 whole, which is shorter than its diff:
```python
import jax
import jax.numpy as jnp
from jax import lax
from jax.sharding import PartitionSpec as P

BLK = 128
V_PARTS = 2


def contract_rows(left, right):
    return lax.dot_general(
        left, right, (((0,), (0,)), ((), ())), preferred_element_type=jnp.float32
    )


def exchange_sum(partial, n_aux):
    sent = partial.astype(jnp.bfloat16)
    if n_aux == 1:
        return sent
    if n_aux == 2:
        other = lax.ppermute(sent, "aux", [(0, 1), (1, 0)])
        return (partial + other.astype(jnp.float32)).astype(jnp.bfloat16)
    return lax.psum(sent, "aux")


def along_line(masked, factors, n_aux):
    me = lax.axis_index("pair")
    middle = (me == 1) | (me == 2)

    def factor(flip):
        return lax.dynamic_index_in_dim(factors, me ^ flip, 0, keepdims=False)

    near = [(z, z ^ 1) for z in range(4)]
    far = [(z, z ^ 2) for z in range(4)]
    inner = [(1, 2), (2, 1)]
    outward = [(2, 3), (1, 0)]
    inward = [(3, 2), (0, 1)]

    width = masked.shape[1] // V_PARTS
    owns = [masked[:, part * width : (part + 1) * width] for part in range(V_PARTS)]
    outs = []
    for own in owns:
        from_far = lax.ppermute(own, "pair", far)
        from_near = lax.ppermute(own, "pair", near)
        from_inner = lax.ppermute(own, "pair", inner)
        from_outer = lax.ppermute(from_far, "pair", outward)
        opposite = jnp.where(middle, from_inner, from_outer)
        partial = contract_rows(own, factor(0))
        partial = partial + contract_rows(from_near, factor(1))
        partial = partial + contract_rows(from_far, factor(2))
        partial = partial + contract_rows(opposite, factor(3))
        coeffs = exchange_sum(partial, n_aux)

        def share(flip):
            return lax.dot_general(
                factor(flip), coeffs, (((1,), (1,)), ((), ())), preferred_element_type=jnp.float32
            )

        share_3 = share(3).astype(jnp.bfloat16)
        got_outer = lax.ppermute(share_3, "pair", inward)
        got_inner = lax.ppermute(share_3, "pair", inner)
        got_near = lax.ppermute(share(1).astype(jnp.bfloat16), "pair", near)
        onward = share(2) + got_outer.astype(jnp.float32)
        got_far = lax.ppermute(onward.astype(jnp.bfloat16), "pair", far)
        response = share(0)
        for got in (got_near, got_inner, got_far):
            response = response + got.astype(jnp.float32)
        outs.append(response)
    return jnp.concatenate(outs, axis=1)


def gathered(masked, factors, n_aux):
    everyone = lax.all_gather(masked, "pair", axis=0, tiled=True)
    rows = factors.reshape(-1, factors.shape[2])
    coeffs = exchange_sum(contract_rows(everyone, rows), n_aux)
    shares = lax.dot_general(
        rows, coeffs, (((1,), (1,)), ((), ())), preferred_element_type=jnp.float32
    )
    return lax.psum_scatter(
        shares.astype(jnp.bfloat16), "pair", scatter_dimension=0, tiled=True
    ).astype(jnp.float32)


def body(n_pair, n_aux, b_built, trial, energy_gap, block_live):
    blocks = trial.shape[0] // BLK
    own_blocks = lax.dynamic_slice_in_dim(block_live, lax.axis_index("aux") * blocks, blocks, 0)
    own_live = jnp.repeat(own_blocks, BLK)
    masked = trial * own_live.astype(jnp.bfloat16)[:, None]
    respond = along_line if n_pair == 4 else gathered
    response = respond(masked, b_built[0], n_aux)
    sigma_out = (
        energy_gap[:, None] * trial.astype(jnp.float32)
        + 2.0 * own_live.astype(jnp.float32)[:, None] * response
    )
    return sigma_out.astype(jnp.bfloat16)


def solution(mesh):
    n_pair, n_aux = mesh.shape["pair"], mesh.shape["aux"]
    return jax.shard_map(
        lambda *args: body(n_pair, n_aux, *args),
        mesh=mesh,
        in_specs=(
            P(("traj", "aux"), None, None, "pair"),
            P(("traj", "pair", "aux"), "root"),
            P(("traj", "pair", "aux")),
            P(("traj", "pair")),
        ),
        out_specs=P(("traj", "pair", "aux"), "root"),
        check_vma=False,
    )
```

time: 334 us -> 94.5 us (0.28)
  blocking collectives: 99.5 us -> 0 us
  waiting for transfers between devices: 114 us -> 43.3 us
  local copies, waits for them, and re-layouts: 62.9 us -> 2.1 us
  other arithmetic: 28.2 us -> 2.94 us
  starting transfers between devices: 5.88 us -> 31.1 us
  between operations: 13.2 us -> 0.33 us
  matrix products: 9.21 us -> 14.2 us
    all_to_all x1 -> x0, blocking collectives: 99.5 us -> none  [body(): lax.all_to_all(b_built, 'pair', split_axis=1, concat_axis=3, tiled=True)]
    all_to_all x1 -> x0, waiting for transfers between devices: 56.5 us -> none  [body(): lax.all_to_all(lax.all_to_all(b_built, 'pair', split_axis=1, concat_axis=...]
    ppermute x0 -> x18, waiting for transfers between devices: none -> 43.3 us  [the longest x2 18.2 us: along_line(): from_far = lax.ppermute(own, 'pair', far)]
    psum x1 -> x0, waiting for transfers between devices: 37.5 us -> none  [body(): coeffs = lax.psum(aux_partial.astype(jnp.bfloat16), 'pair')]
    all_to_all x2 -> x0, local copies, waits for them, and re-layouts: 34.8 us -> none  [the longest x1 28.6 us: body(): lax.all_to_all(b_built, 'pair', split_axis=1, concat_axis=3, tiled=True)]
    ppermute x0 -> x18, starting transfers between devices: none -> 31.1 us  [the longest x2 9 us: along_line(): got_outer = lax.ppermute(share_3, 'pair', inward)]
    unnamed x12 -> x9, local copies, waits for them, and re-layouts: 27.1 us -> 0.92 us
    unnamed x1 -> x0, other arithmetic: 26 us -> none
  transfers between devices with their start and end apart: 4 -> 18, of which waited for: 3 -> 8; matrix products, arithmetic and copies ran while one was open for 6% -> 14% of each run, Pallas kernels for 0% -> 0%
where the time goes in v2:
time: 94.5 us; the launch traced here: 94 us
  waiting for transfers between devices  43.3 us (46%)
  starting transfers between devices  31.1 us (33%)
  matrix products  14.2 us (15%)
  other arithmetic  2.94 us (3%)
  local copies, waits for them, and re-layouts  2.1 us (2%)
    ppermute x2, waiting for transfers between devices, along_line(): from_far = lax.ppermute(own, 'pair', far)  18.2 us
    ppermute x2, waiting for transfers between devices, along_line(): got_far = lax.ppermute(onward.astype(jnp.bfloat16), 'pair', far)  11.5 us
    ppermute x2, starting transfers between devices, along_line(): got_outer = lax.ppermute(share_3, 'pair', inward)  9 us
    ppermute x2, waiting for transfers between devices, along_line(): got_near = lax.ppermute(share(1).astype(jnp.bfloat16), 'pair', near)  8.01 us
    dot_general x8, matrix products, contract_rows(): lax.dot_general(left, right, (((0,), (0,)), ((), ())), preferred_element_...  7.72 us
    ppermute x2, starting transfers between devices, along_line(): from_far = lax.ppermute(own, 'pair', far)  7.31 us
    dot_general x8, matrix products, share(): lax.dot_general(factor(flip), coeffs, (((1,), (1,)), ((), ())), preferred...  6.48 us
    ppermute x2, starting transfers between devices, exchange_sum(): other = lax.ppermute(sent, 'aux', [(0, 1), (1, 0)])  3.52 us
  transfers between devices with their start and end apart: 18, of which 8 were waited for; matrix products, arithmetic and copies ran while one was open for 14% of the time, Pallas kernels for 0%

profile of v2, /device:TPU:0, one launch (start us, length us, event | category | flops | bytes accessed | tf_op | source)
XLA Modules:
  0.0 94.0 jit_solution(5831693188379284596)
XLA Ops:
  0.0 0.7 dynamic-slice_convert_fusion
  0.7 0.1 broadcast_bitcast_fusion.1
  0.8 1.2 %broadcast_multiply_fusion = bf16[1024,256]{1,0:T(8,128)(2,1)S(1)} fusion(bf16[1024,256]{1,0:T(8,128)(2,1)} %param.5, bf16[1024]{0:T(1024)(128)(2,1)S(1)} %broadcast_bitcast_fusion.1), kind=kLoop, calls=%fused_computation.61 | loop fusion | flops 262144 | bytes 1050624 | tf_op jit(solution)/shard_map/mul | solution.py:88
  2.1 4.1 %collective-permute-start.1 = (bf16[1024,128]{1,0:T(8,128)(2,1)S(1)}, bf16[1024,128]{1,0:T(8,128)(2,1)S(1)}, u32[]{:S(2)}, u32[]{:S(2)}) collective-permute-start(bf16[1024,128]{1,0:T(8,128)(2,1)S(1)} %get-tuple-element.5), channel_id=1, source_target_pairs={{0,8},{4,12},{8,0},{12,4},{1,9},{5,13},{9,1},{13,5},{2,10},{6,14},... | collective-permute-start | bytes 786440 | tf_op jit(solution)/shard_map/ppermute | solution.py:43
  6.2 1.6 %collective-permute-start = (bf16[1024,128]{1,0:T(8,128)(2,1)S(1)}, bf16[1024,128]{1,0:T(8,128)(2,1)S(1)}, u32[]{:S(2)}, u32[]{:S(2)}) collective-permute-start(bf16[1024,128]{1,0:T(8,128)(2,1)S(1)} %get-tuple-element.5), channel_id=1, source_target_pairs={{0,4},{4,0},{8,12},{12,8},{1,5},{5,1},{9,13},{13,9},{2,6},{6,2},{1... | collective-permute-start | bytes 786440 | tf_op jit(solution)/shard_map/ppermute | solution.py:44
  7.8 0.7 collective-permute-start.2
  8.4 3.2 %collective-permute-start.10 = (bf16[1024,128]{1,0:T(8,128)(2,1)S(1)}, bf16[1024,128]{1,0:T(8,128)(2,1)S(1)}, u32[]{:S(2)}, u32[]{:S(2)}) collective-permute-start(bf16[1024,128]{1,0:T(8,128)(2,1)S(1)} %get-tuple-element.6), channel_id=1, source_target_pairs={{0,8},{4,12},{8,0},{12,4},{1,9},{5,13},{9,1},{13,5},{2,10},{6,14},... | collective-permute-start | bytes 786440 | tf_op jit(solution)/shard_map/ppermute | solution.py:43
  11.7 0.0 collective-permute-start.9
  11.7 1.5 %fusion.21 = f32[128,512]{1,0:T(8,128)S(1)} fusion(bf16[1,4,1024,512]{3,2,1,0:T(8,128)(2,1)} %param.4, s32[]{:T(128)S(6)} %select_n.41, bf16[1024,256]{1,0:T(8,128)(2,1)S(1)} %broadcast_multiply_fusion), kind=kOutput, calls=%fused_computation.36 | convolution fusion | flops 134217728 | bytes 1572868 | tf_op jit(solution)/shard_map/dot_general | solution.py:11
  13.2 0.7 convert_multiply_fusion
  14.0 1.7 %fusion.24 = f32[128,512]{1,0:T(8,128)S(1)} fusion(bf16[1,4,1024,512]{3,2,1,0:T(8,128)(2,1)} %param.4, s32[]{:T(128)S(6)} %select_n.41, bf16[1024,256]{1,0:T(8,128)(2,1)S(1)} %broadcast_multiply_fusion), kind=kOutput, calls=%fused_computation.39 | convolution fusion | flops 134217728 | bytes 1572868 | tf_op jit(solution)/shard_map/dot_general | solution.py:11
  15.7 4.2 %collective-permute-done.1 = bf16[1024,128]{1,0:T(8,128)(2,1)S(1)} collective-permute-done((bf16[1024,128]{1,0:T(8,128)(2,1)S(1)}, bf16[1024,128]{1,0:T(8,128)(2,1)S(1)}, u32[]{:S(2)}, u32[]{:S(2)}) %collective-permute-start.1) | collective-permute-done | bytes 262176 | tf_op jit(solution)/shard_map/ppermute | solution.py:43
  19.9 0.7 collective-permute-start.11
  20.5 0.0 collective-permute-done
  20.5 1.3 %collective-permute-start.3 = (bf16[1024,128]{1,0:T(8,128)(2,1)S(1)}, bf16[1024,128]{1,0:T(8,128)(2,1)S(1)}, u32[]{:S(2)}, u32[]{:S(2)}) collective-permute-start(bf16[1024,128]{1,0:T(8,128)(2,1)S(1)} %collective-permute-done.1), channel_id=1, source_target_pairs={{8,12},{4,0},{9,13},{5,1},{10,14},{6,2},{11,15},{7,3},{24,28},{20,... | collective-permute-start | bytes 786440 | tf_op jit(solution)/shard_map/ppermute | solution.py:46
  21.8 14.0 %collective-permute-done.10 = bf16[1024,128]{1,0:T(8,128)(2,1)S(1)} collective-permute-done((bf16[1024,128]{1,0:T(8,128)(2,1)S(1)}, bf16[1024,128]{1,0:T(8,128)(2,1)S(1)}, u32[]{:S(2)}, u32[]{:S(2)}) %collective-permute-start.10) | collective-permute-done | bytes 262176 | tf_op jit(solution)/shard_map/ppermute | solution.py:43
  35.9 1.3 %collective-permute-start.12 = (bf16[1024,128]{1,0:T(8,128)(2,1)S(1)}, bf16[1024,128]{1,0:T(8,128)(2,1)S(1)}, u32[]{:S(2)}, u32[]{:S(2)}) collective-permute-start(bf16[1024,128]{1,0:T(8,128)(2,1)S(1)} %collective-permute-done.10), channel_id=1, source_target_pairs={{8,12},{4,0},{9,13},{5,1},{10,14},{6,2},{11,15},{7,3},{24,28},{20,... | collective-permute-start | bytes 786440 | tf_op jit(solution)/shard_map/ppermute | solution.py:46
  37.2 1.6 %convolution_add_fusion.9 = f32[128,512]{1,0:T(8,128)S(1)} fusion(f32[128,512]{1,0:T(8,128)S(1)} %fusion.24, bf16[1024,128]{1,0:T(8,128)(2,1)S(1)} %collective-permute-done, bf16[1,4,1024,512]{3,2,1,0:T(8,128)(2,1)} %param.4, s32[]{:T(128)S(6)} %select_n.42), kind=kOutput, calls=%fused_computation.19 | convolution fusion | flops 134283264 | bytes 1835012 | tf_op jit(solution)/shard_map/dot_general | solution.py:11
  38.7 1.6 %convolution_add_fusion.8 = f32[128,512]{1,0:T(8,128)S(1)} fusion(f32[128,512]{1,0:T(8,128)S(1)} %convolution_add_fusion.9, bf16[1024,128]{1,0:T(8,128)(2,1)S(1)} %collective-permute-done.1, bf16[1,4,1024,512]{3,2,1,0:T(8,128)(2,1)} %param.4, s32[]{:T(128)S(6)} %select_n.43), kind=kOutput, calls=%fused_computation.18 | convolution fusion | flops 134283264 | bytes 1835012 | tf_op jit(solution)/shard_map/dot_general | solution.py:11
  40.3 0.0 collective-permute-done.9
  40.3 0.3 convolution_add_fusion.6
  40.7 0.3 convolution_add_fusion.5
  41.0 0.0 collective-permute-done.2
  41.0 0.0 collective-permute-done.3
  41.0 0.3 fusion.66
  41.4 1.9 %collective-permute-start.4 = (bf16[128,512]{1,0:T(8,128)(2,1)S(1)}, bf16[128,512]{1,0:T(8,128)(2,1)S(1)}, u32[]{:S(2)}, u32[]{:S(2)}) collective-permute-start(bf16[128,512]{1,0:T(8,128)(2,1)S(1)} %get-tuple-element.9), channel_id=1, source_target_pairs={{0,2},{2,0},{1,3},{3,1},{4,6},{6,4},{5,7},{7,5},{8,10},{10,8},{9,1... | collective-permute-start | bytes 393224 | tf_op jit(solution)/shard_map/ppermute | solution.py:21
  43.3 0.0 collective-permute-done.11
  43.3 1.1 %collective-permute-done.12 = bf16[1024,128]{1,0:T(8,128)(2,1)S(1)} collective-permute-done((bf16[1024,128]{1,0:T(8,128)(2,1)S(1)}, bf16[1024,128]{1,0:T(8,128)(2,1)S(1)}, u32[]{:S(2)}, u32[]{:S(2)}) %collective-permute-start.12) | collective-permute-done | bytes 262176 | tf_op jit(solution)/shard_map/ppermute | solution.py:46
  44.4 0.3 fusion.65
  44.8 1.6 %collective-permute-start.13 = (bf16[128,512]{1,0:T(8,128)(2,1)S(1)}, bf16[128,512]{1,0:T(8,128)(2,1)S(1)}, u32[]{:S(2)}, u32[]{:S(2)}) collective-permute-start(bf16[128,512]{1,0:T(8,128)(2,1)S(1)} %get-tuple-element.7), channel_id=1, source_target_pairs={{0,2},{2,0},{1,3},{3,1},{4,6},{6,4},{5,7},{7,5},{8,10},{10,8},{9,1... | collective-permute-start | bytes 393224 | tf_op jit(solution)/shard_map/ppermute | solution.py:21
  46.4 1.4 %collective-permute-done.4 = bf16[128,512]{1,0:T(8,128)(2,1)S(1)} collective-permute-done((bf16[128,512]{1,0:T(8,128)(2,1)S(1)}, bf16[128,512]{1,0:T(8,128)(2,1)S(1)}, u32[]{:S(2)}, u32[]{:S(2)}) %collective-permute-start.4) | collective-permute-done | bytes 131104 | tf_op jit(solution)/shard_map/ppermute | solution.py:21
  47.8 0.5 convolution_convert_fusion.2
  48.3 0.0 copy-start.1
  48.3 3.4 %collective-permute-start.7 = (bf16[1024,128]{0,1:T(8,128)(2,1)S(1)}, bf16[1024,128]{0,1:T(8,128)(2,1)S(1)}, u32[]{:S(2)}, u32[]{:S(2)}) collective-permute-start(bf16[1024,128]{0,1:T(8,128)(2,1)S(1)} %convolution_convert_fusion.2), channel_id=1, source_target_pairs={{12,8},{0,4},{13,9},{1,5},{14,10},{2,6},{15,11},{3,7},{28,24},{16,... | collective-permute-start | bytes 786440 | tf_op jit(solution)/shard_map/ppermute | solution.py:60
  51.7 0.7 collective-permute-start.6
  52.4 0.5 convolution_convert_fusion.3
  52.9 0.0 collective-permute-done.13
  52.9 0.5 convolution_convert_fusion
  53.4 5.6 %collective-permute-start.16 = (bf16[1024,128]{0,1:T(8,128)(2,1)S(1)}, bf16[1024,128]{0,1:T(8,128)(2,1)S(1)}, u32[]{:S(2)}, u32[]{:S(2)}) collective-permute-start(bf16[1024,128]{0,1:T(8,128)(2,1)S(1)} %convolution_convert_fusion), channel_id=1, source_target_pairs={{12,8},{0,4},{13,9},{1,5},{14,10},{2,6},{15,11},{3,7},{28,24},{16,... | collective-permute-start | bytes 786440 | tf_op jit(solution)/shard_map/ppermute | solution.py:60
  59.1 0.5 convolution_convert_fusion.1
  59.5 0.7 collective-permute-start.15
  60.2 0.7 collective-permute-start.5
  60.9 0.0 collective-permute-done.7
  60.9 1.4 %collective-permute-start.14 = (bf16[1024,128]{0,1:T(8,128)(2,1)S(1)}, bf16[1024,128]{0,1:T(8,128)(2,1)S(1)}, u32[]{:S(2)}, u32[]{:S(2)}) collective-permute-start(bf16[1024,128]{0,1:T(8,128)(2,1)S(1)} %convolution_convert_fusion.1), channel_id=1, source_target_pairs={{0,4},{4,0},{8,12},{12,8},{1,5},{5,1},{9,13},{13,9},{2,6},{6,2},{1... | collective-permute-start | bytes 786440 | tf_op jit(solution)/shard_map/ppermute | solution.py:62
  62.3 0.5 fusion.4
  62.8 0.0 copy-start.3
  62.8 3.0 %collective-permute-done.16 = bf16[1024,128]{0,1:T(8,128)(2,1)S(1)} collective-permute-done((bf16[1024,128]{0,1:T(8,128)(2,1)S(1)}, bf16[1024,128]{0,1:T(8,128)(2,1)S(1)}, u32[]{:S(2)}, u32[]{:S(2)}) %collective-permute-start.16) | collective-permute-done | bytes 262176 | tf_op jit(solution)/shard_map/ppermute | solution.py:60
  65.8 2.4 %collective-permute-start.8 = (bf16[1024,128]{0,1:T(8,128)(2,1)S(1)}, bf16[1024,128]{0,1:T(8,128)(2,1)}, u32[]{:S(2)}, u32[]{:S(2)}) collective-permute-start(bf16[1024,128]{0,1:T(8,128)(2,1)S(1)} %fusion.4), channel_id=1, source_target_pairs={{0,8},{4,12},{8,0},{12,4},{1,9},{5,13},{9,1},{13,5},{2,10},{6,14},... | collective-permute-start | bytes 786440 | tf_op jit(solution)/shard_map/ppermute | solution.py:64
  68.2 0.5 fusion.5
  68.6 8.0 %collective-permute-done.5 = bf16[1024,128]{0,1:T(8,128)(2,1)S(1)} collective-permute-done((bf16[1024,128]{0,1:T(8,128)(2,1)S(1)}, bf16[1024,128]{0,1:T(8,128)(2,1)S(1)}, u32[]{:S(2)}, u32[]{:S(2)}) %collective-permute-start.5) | collective-permute-done | bytes 262176 | tf_op jit(solution)/shard_map/ppermute | solution.py:62
  76.6 0.0 collective-permute-start.17
  76.6 0.7 copy-done.2
  77.3 0.1 broadcast_bitcast_fusion
  77.4 0.0 copy-done.1
  77.4 0.2 copy.5
  77.6 0.0 collective-permute-done.6
  77.6 4.1 %collective-permute-done.8 = bf16[1024,128]{0,1:T(8,128)(2,1)} collective-permute-done((bf16[1024,128]{0,1:T(8,128)(2,1)S(1)}, bf16[1024,128]{0,1:T(8,128)(2,1)}, u32[]{:S(2)}, u32[]{:S(2)}) %collective-permute-start.8) | collective-permute-done | bytes 262176 | tf_op jit(solution)/shard_map/ppermute | solution.py:64
  81.8 1.8 %fusion.1 = f32[1024,128]{0,1:T(8,128)S(1)} fusion(bf16[128,512]{1,0:T(8,128)(2,1)S(1)} %add_convert_fusion.1, bf16[1,4,1024,512]{3,2,1,0:T(8,128)(2,1)} %param.4, s32[]{:T(128)S(6)} %select_n.41, bf16[1024,128]{0,1:T(8,128)(2,1)} %collective-permute-done.8, bf16[1024,128]{0,1:T(8,128)(2,1)S(1)} %collective-permute-done.6, bf16[1024,128]{0,1:T(8,128)(2,1)} %copy-done.2), kind=kOutput, calls=%fused_computation.5 | convolution fusion | flops 135004160 | bytes 2490372 | tf_op jit(solution)/shard_map/dot_general | solution.py:55
  83.6 0.0 collective-permute-done.14
  83.6 0.0 collective-permute-done.15
  83.6 7.4 %collective-permute-done.17 = bf16[1024,128]{0,1:T(8,128)(2,1)} collective-permute-done((bf16[1024,128]{0,1:T(8,128)(2,1)S(1)}, bf16[1024,128]{0,1:T(8,128)(2,1)}, u32[]{:S(2)}, u32[]{:S(2)}) %collective-permute-start.17) | collective-permute-done | bytes 262176 | tf_op jit(solution)/shard_map/ppermute | solution.py:64
  91.0 1.8 %fusion.3 = f32[1024,128]{0,1:T(8,128)S(1)} fusion(bf16[128,512]{1,0:T(8,128)(2,1)S(1)} %add_convert_fusion, bf16[1,4,1024,512]{3,2,1,0:T(8,128)(2,1)} %param.4, s32[]{:T(128)S(6)} %select_n.41, bf16[1024,128]{0,1:T(8,128)(2,1)} %collective-permute-done.17, bf16[1024,128]{0,1:T(8,128)(2,1)S(1)} %collective-permute-done.15, ...), kind=kOutput, calls=%fused_computation.7 | convolution fusion | flops 135004160 | bytes 2490372 | tf_op jit(solution)/shard_map/dot_general | solution.py:55
  92.8 0.2 fusion.7
  93.0 1.0 %copy.12 = bf16[1024,256]{1,0:T(8,128)(2,1)} copy(bf16[1024,256]{0,1:T(8,128)(2,1)S(1)} %fusion.7) | data formatting | bytes 1048576 | tf_op jit(solution)/shard_map/convert_element_type | solution.py:95
  (7 shorter events, 0.1 us)
Async XLA Ops:
  2.1 17.8 %collective-permute-start.1 = (bf16[1024,128]{1,0:T(8,128)(2,1)S(1)}, bf16[1024,128]{1,0:T(8,128)(2,1)S(1)}, u32[]{:S(2)}, u32[]{:S(2)}) collective-permute-start(bf16[1024,128]{1,0:T(8,128)(2,1)S(1)} %get-tuple-element.5), channel_id=1, source_target_pairs={{0,8},{4,12},{8,0},{12,4},{1,9},{5,13},{9,1},{13,5},{2,10},{6,14},... | collective-permute-start | bytes 786440 | tf_op jit(solution)/shard_map/ppermute | solution.py:43
  6.2 14.3 %collective-permute-start = (bf16[1024,128]{1,0:T(8,128)(2,1)S(1)}, bf16[1024,128]{1,0:T(8,128)(2,1)S(1)}, u32[]{:S(2)}, u32[]{:S(2)}) collective-permute-start(bf16[1024,128]{1,0:T(8,128)(2,1)S(1)} %get-tuple-element.5), channel_id=1, source_target_pairs={{0,4},{4,0},{8,12},{12,8},{1,5},{5,1},{9,13},{13,9},{2,6},{6,2},{1... | collective-permute-start | bytes 786440 | tf_op jit(solution)/shard_map/ppermute | solution.py:44
  7.8 33.2 %collective-permute-start.2 = (bf16[1024,128]{1,0:T(8,128)(2,1)S(1)}, bf16[1024,128]{1,0:T(8,128)(2,1)S(1)}, u32[]{:S(2)}, u32[]{:S(2)}) collective-permute-start(bf16[1024,128]{1,0:T(8,128)(2,1)S(1)} %get-tuple-element.5), channel_id=1, source_target_pairs={{4,8},{8,4},{5,9},{9,5},{6,10},{10,6},{7,11},{11,7},{20,24},{24,20... | collective-permute-start | bytes 786440 | tf_op jit(solution)/shard_map/ppermute | solution.py:45
  8.4 27.4 %collective-permute-start.10 = (bf16[1024,128]{1,0:T(8,128)(2,1)S(1)}, bf16[1024,128]{1,0:T(8,128)(2,1)S(1)}, u32[]{:S(2)}, u32[]{:S(2)}) collective-permute-start(bf16[1024,128]{1,0:T(8,128)(2,1)S(1)} %get-tuple-element.6), channel_id=1, source_target_pairs={{0,8},{4,12},{8,0},{12,4},{1,9},{5,13},{9,1},{13,5},{2,10},{6,14},... | collective-permute-start | bytes 786440 | tf_op jit(solution)/shard_map/ppermute | solution.py:43
  11.7 28.7 %collective-permute-start.9 = (bf16[1024,128]{1,0:T(8,128)(2,1)S(1)}, bf16[1024,128]{1,0:T(8,128)(2,1)S(1)}, u32[]{:S(2)}, u32[]{:S(2)}) collective-permute-start(bf16[1024,128]{1,0:T(8,128)(2,1)S(1)} %get-tuple-element.6), channel_id=1, source_target_pairs={{0,4},{4,0},{8,12},{12,8},{1,5},{5,1},{9,13},{13,9},{2,6},{6,2},{1... | collective-permute-start | bytes 786440 | tf_op jit(solution)/shard_map/ppermute | solution.py:44
  14.0 26.4 %copy-start = (bf16[1,4,1024,512]{3,2,1,0:T(8,128)(2,1)S(1)}, bf16[1,4,1024,512]{3,2,1,0:T(8,128)(2,1)}, u32[]{:S(2)}) copy-start(bf16[1,4,1024,512]{3,2,1,0:T(8,128)(2,1)} %param.4) | copy-start | bytes 12582916
  19.9 23.4 %collective-permute-start.11 = (bf16[1024,128]{1,0:T(8,128)(2,1)S(1)}, bf16[1024,128]{1,0:T(8,128)(2,1)S(1)}, u32[]{:S(2)}, u32[]{:S(2)}) collective-permute-start(bf16[1024,128]{1,0:T(8,128)(2,1)S(1)} %get-tuple-element.6), channel_id=1, source_target_pairs={{4,8},{8,4},{5,9},{9,5},{6,10},{10,6},{7,11},{11,7},{20,24},{24,20... | collective-permute-start | bytes 786440 | tf_op jit(solution)/shard_map/ppermute | solution.py:45
  20.5 20.5 %collective-permute-start.3 = (bf16[1024,128]{1,0:T(8,128)(2,1)S(1)}, bf16[1024,128]{1,0:T(8,128)(2,1)S(1)}, u32[]{:S(2)}, u32[]{:S(2)}) collective-permute-start(bf16[1024,128]{1,0:T(8,128)(2,1)S(1)} %collective-permute-done.1), channel_id=1, source_target_pairs={{8,12},{4,0},{9,13},{5,1},{10,14},{6,2},{11,15},{7,3},{24,28},{20,... | collective-permute-start | bytes 786440 | tf_op jit(solution)/shard_map/ppermute | solution.py:46
  35.9 8.5 %collective-permute-start.12 = (bf16[1024,128]{1,0:T(8,128)(2,1)S(1)}, bf16[1024,128]{1,0:T(8,128)(2,1)S(1)}, u32[]{:S(2)}, u32[]{:S(2)}) collective-permute-start(bf16[1024,128]{1,0:T(8,128)(2,1)S(1)} %collective-permute-done.10), channel_id=1, source_target_pairs={{8,12},{4,0},{9,13},{5,1},{10,14},{6,2},{11,15},{7,3},{24,28},{20,... | collective-permute-start | bytes 786440 | tf_op jit(solution)/shard_map/ppermute | solution.py:46
  41.4 6.4 %collective-permute-start.4 = (bf16[128,512]{1,0:T(8,128)(2,1)S(1)}, bf16[128,512]{1,0:T(8,128)(2,1)S(1)}, u32[]{:S(2)}, u32[]{:S(2)}) collective-permute-start(bf16[128,512]{1,0:T(8,128)(2,1)S(1)} %get-tuple-element.9), channel_id=1, source_target_pairs={{0,2},{2,0},{1,3},{3,1},{4,6},{6,4},{5,7},{7,5},{8,10},{10,8},{9,1... | collective-permute-start | bytes 393224 | tf_op jit(solution)/shard_map/ppermute | solution.py:21
  44.8 8.1 %collective-permute-start.13 = (bf16[128,512]{1,0:T(8,128)(2,1)S(1)}, bf16[128,512]{1,0:T(8,128)(2,1)S(1)}, u32[]{:S(2)}, u32[]{:S(2)}) collective-permute-start(bf16[128,512]{1,0:T(8,128)(2,1)S(1)} %get-tuple-element.7), channel_id=1, source_target_pairs={{0,2},{2,0},{1,3},{3,1},{4,6},{6,4},{5,7},{7,5},{8,10},{10,8},{9,1... | collective-permute-start | bytes 393224 | tf_op jit(solution)/shard_map/ppermute | solution.py:21
  48.3 29.1 %copy-start.1 = (bf16[1024,256]{1,0:T(8,128)(2,1)S(1)}, bf16[1024,256]{1,0:T(8,128)(2,1)}, u32[]{:S(2)}) copy-start(bf16[1024,256]{1,0:T(8,128)(2,1)} %param.5) | copy-start | bytes 1572868
  48.3 12.6 %collective-permute-start.7 = (bf16[1024,128]{0,1:T(8,128)(2,1)S(1)}, bf16[1024,128]{0,1:T(8,128)(2,1)S(1)}, u32[]{:S(2)}, u32[]{:S(2)}) collective-permute-start(bf16[1024,128]{0,1:T(8,128)(2,1)S(1)} %convolution_convert_fusion.2), channel_id=1, source_target_pairs={{12,8},{0,4},{13,9},{1,5},{14,10},{2,6},{15,11},{3,7},{28,24},{16,... | collective-permute-start | bytes 786440 | tf_op jit(solution)/shard_map/ppermute | solution.py:60
  51.7 25.9 %collective-permute-start.6 = (bf16[1024,128]{0,1:T(8,128)(2,1)S(1)}, bf16[1024,128]{0,1:T(8,128)(2,1)S(1)}, u32[]{:S(2)}, u32[]{:S(2)}) collective-permute-start(bf16[1024,128]{0,1:T(8,128)(2,1)S(1)} %convolution_convert_fusion.2), channel_id=1, source_target_pairs={{4,8},{8,4},{5,9},{9,5},{6,10},{10,6},{7,11},{11,7},{20,24},{24,20... | collective-permute-start | bytes 786440 | tf_op jit(solution)/shard_map/ppermute | solution.py:61
  53.4 12.4 %collective-permute-start.16 = (bf16[1024,128]{0,1:T(8,128)(2,1)S(1)}, bf16[1024,128]{0,1:T(8,128)(2,1)S(1)}, u32[]{:S(2)}, u32[]{:S(2)}) collective-permute-start(bf16[1024,128]{0,1:T(8,128)(2,1)S(1)} %convolution_convert_fusion), channel_id=1, source_target_pairs={{12,8},{0,4},{13,9},{1,5},{14,10},{2,6},{15,11},{3,7},{28,24},{16,... | collective-permute-start | bytes 786440 | tf_op jit(solution)/shard_map/ppermute | solution.py:60
  59.5 24.1 %collective-permute-start.15 = (bf16[1024,128]{0,1:T(8,128)(2,1)S(1)}, bf16[1024,128]{0,1:T(8,128)(2,1)S(1)}, u32[]{:S(2)}, u32[]{:S(2)}) collective-permute-start(bf16[1024,128]{0,1:T(8,128)(2,1)S(1)} %convolution_convert_fusion), channel_id=1, source_target_pairs={{4,8},{8,4},{5,9},{9,5},{6,10},{10,6},{7,11},{11,7},{20,24},{24,20... | collective-permute-start | bytes 786440 | tf_op jit(solution)/shard_map/ppermute | solution.py:61
  60.2 16.4 %collective-permute-start.5 = (bf16[1024,128]{0,1:T(8,128)(2,1)S(1)}, bf16[1024,128]{0,1:T(8,128)(2,1)S(1)}, u32[]{:S(2)}, u32[]{:S(2)}) collective-permute-start(bf16[1024,128]{0,1:T(8,128)(2,1)S(1)} %convolution_convert_fusion.3), channel_id=1, source_target_pairs={{0,4},{4,0},{8,12},{12,8},{1,5},{5,1},{9,13},{13,9},{2,6},{6,2},{1... | collective-permute-start | bytes 786440 | tf_op jit(solution)/shard_map/ppermute | solution.py:62
  60.9 22.7 %collective-permute-start.14 = (bf16[1024,128]{0,1:T(8,128)(2,1)S(1)}, bf16[1024,128]{0,1:T(8,128)(2,1)S(1)}, u32[]{:S(2)}, u32[]{:S(2)}) collective-permute-start(bf16[1024,128]{0,1:T(8,128)(2,1)S(1)} %convolution_convert_fusion.1), channel_id=1, source_target_pairs={{0,4},{4,0},{8,12},{12,8},{1,5},{5,1},{9,13},{13,9},{2,6},{6,2},{1... | collective-permute-start | bytes 786440 | tf_op jit(solution)/shard_map/ppermute | solution.py:62
  62.8 30.0 %copy-start.3 = (f32[1024]{0:T(1024)S(1)}, f32[1024]{0:T(1024)}, u32[]{:S(2)}) copy-start(f32[1024]{0:T(1024)} %param.6) | copy-start | bytes 12292
  65.8 16.0 %collective-permute-start.8 = (bf16[1024,128]{0,1:T(8,128)(2,1)S(1)}, bf16[1024,128]{0,1:T(8,128)(2,1)}, u32[]{:S(2)}, u32[]{:S(2)}) collective-permute-start(bf16[1024,128]{0,1:T(8,128)(2,1)S(1)} %fusion.4), channel_id=1, source_target_pairs={{0,8},{4,12},{8,0},{12,4},{1,9},{5,13},{9,1},{13,5},{2,10},{6,14},... | collective-permute-start | bytes 786440 | tf_op jit(solution)/shard_map/ppermute | solution.py:64
  76.6 0.7 copy-start.2
  76.6 14.4 %collective-permute-start.17 = (bf16[1024,128]{0,1:T(8,128)(2,1)S(1)}, bf16[1024,128]{0,1:T(8,128)(2,1)}, u32[]{:S(2)}, u32[]{:S(2)}) collective-permute-start(bf16[1024,128]{0,1:T(8,128)(2,1)S(1)} %fusion.5), channel_id=1, source_target_pairs={{0,8},{4,12},{8,0},{12,4},{1,9},{5,13},{9,1},{13,5},{2,10},{6,14},... | collective-permute-start | bytes 786440 | tf_op jit(solution)/shard_map/ppermute | solution.py:64

commit v3 on v2

v3 whole, which is shorter than its diff:
```python
import functools

import jax
import jax.numpy as jnp
from jax import lax
from jax.experimental import pallas as pl
from jax.experimental.pallas import tpu as pltpu
from jax.sharding import PartitionSpec as P

BLK = 128
V_PARTS = 2

SMEM = pl.BlockSpec(memory_space=pltpu.SMEM)
VMEM = pl.BlockSpec(memory_space=pltpu.VMEM)
ANY = pl.BlockSpec(memory_space=pl.ANY)


def contract_rows(left, right):
    return lax.dot_general(
        left, right, (((0,), (0,)), ((), ())), preferred_element_type=jnp.float32
    )


def exchange_sum(partial, n_aux):
    sent = partial.astype(jnp.bfloat16)
    if n_aux == 1:
        return sent
    if n_aux == 2:
        other = lax.ppermute(sent, "aux", [(0, 1), (1, 0)])
        return (partial + other.astype(jnp.float32)).astype(jnp.bfloat16)
    return lax.psum(sent, "aux")


def block_rows(block):
    return pl.ds(pl.multiple_of(block * BLK, BLK), BLK)


def pack_trial_kernel(live_ref, trial_ref, *out_refs):
    width = out_refs[0].shape[1]
    for out in out_refs:
        out[...] = jnp.zeros_like(out)
    slot = jnp.int32(0)
    for block in range(trial_ref.shape[0] // BLK):
        here = live_ref[0, block]

        @pl.when(here > 0)
        def _(slot=slot, block=block):
            for part, out in enumerate(out_refs):
                out[block_rows(slot), :] = trial_ref[
                    pl.ds(block * BLK, BLK), pl.ds(part * width, width)
                ]

        slot = slot + here


def pack_factors_kernel(slots, live_ref, me_ref, factors_ref, out_ref, index_ref, sems):
    pairs, blocks = live_ref.shape
    copies = []
    for flip in range(pairs):
        for slot in range(blocks):
            index_ref[flip, slot] = 0
        at = jnp.int32(0)
        for block in range(blocks):
            index_ref[flip, at] = block
            at = at + live_ref[flip, block]
        for slot in range(slots):
            copies.append(
                pltpu.make_async_copy(
                    factors_ref.at[me_ref[0] ^ flip, block_rows(index_ref[flip, slot]), :],
                    out_ref.at[flip, pl.ds(slot * BLK, BLK), :],
                    sems.at[flip, slot],
                )
            )
            copies[-1].start()
    for copy in copies:
        copy.wait()


def unpack_kernel(live_ref, base_ref, own_ref, near_ref, inner_ref, far_ref, before_ref, out_ref):
    del before_ref
    slot = jnp.int32(0)
    for block in range(out_ref.shape[0] // BLK):
        rows = pl.ds(block * BLK, BLK)
        here = live_ref[0, block]

        @pl.when(here > 0)
        def _(slot=slot, rows=rows):
            at = block_rows(slot)
            response = own_ref[at, :]
            for ref in (near_ref, inner_ref, far_ref):
                response = response + ref[at, :].astype(jnp.float32)
            out_ref[rows, :] = (base_ref[rows, :] + 2.0 * response).astype(out_ref.dtype)

        @pl.when(here == 0)
        def _(rows=rows):
            out_ref[rows, :] = base_ref[rows, :].astype(out_ref.dtype)

        slot = slot + here


def along_line(slots, n_aux, live, trial, factors, base):
    me = lax.axis_index("pair")
    middle = (me == 1) | (me == 2)
    rows, vecs = trial.shape
    width = vecs // V_PARTS
    aux_here = factors.shape[2]
    near = [(z, z ^ 1) for z in range(4)]
    far = [(z, z ^ 2) for z in range(4)]
    inner = [(1, 2), (2, 1)]
    outward = [(2, 3), (1, 0)]
    inward = [(3, 2), (0, 1)]

    owns = pl.pallas_call(
        pack_trial_kernel,
        out_shape=[jax.ShapeDtypeStruct((slots * BLK, width), trial.dtype)] * V_PARTS,
        in_specs=[SMEM, VMEM],
        out_specs=[VMEM] * V_PARTS,
        name="pack_trial",
    )(live, trial)
    packed = pl.pallas_call(
        functools.partial(pack_factors_kernel, slots),
        out_shape=jax.ShapeDtypeStruct((4, slots * BLK, aux_here), factors.dtype),
        in_specs=[SMEM, SMEM, ANY],
        out_specs=ANY,
        scratch_shapes=[
            pltpu.SMEM((4, rows // BLK), jnp.int32),
            pltpu.SemaphoreType.DMA((4, slots)),
        ],
        name="pack_factors",
    )(live, me.astype(jnp.int32).reshape(1), factors)

    sigma = None
    for part, own in enumerate(owns):
        from_far = lax.ppermute(own, "pair", far)
        from_near = lax.ppermute(own, "pair", near)
        from_inner = lax.ppermute(own, "pair", inner)
        from_outer = lax.ppermute(from_far, "pair", outward)
        opposite = jnp.where(middle, from_inner, from_outer)
        partial = contract_rows(own, packed[0])
        partial = partial + contract_rows(from_near, packed[1])
        partial = partial + contract_rows(from_far, packed[2])
        partial = partial + contract_rows(opposite, packed[3])
        coeffs = exchange_sum(partial, n_aux)

        def share(flip):
            return lax.dot_general(
                packed[flip], coeffs, (((1,), (1,)), ((), ())), preferred_element_type=jnp.float32
            )

        share_3 = share(3).astype(jnp.bfloat16)
        got_outer = lax.ppermute(share_3, "pair", inward)
        got_inner = lax.ppermute(share_3, "pair", inner)
        got_near = lax.ppermute(share(1).astype(jnp.bfloat16), "pair", near)
        onward = share(2) + got_outer.astype(jnp.float32)
        got_far = lax.ppermute(onward.astype(jnp.bfloat16), "pair", far)
        half = pl.BlockSpec((rows, width), lambda _, part=part: (0, part))
        whole = [pl.BlockSpec((slots * BLK, width), lambda _: (0, 0))] * 4
        first = sigma is None
        sigma = pl.pallas_call(
            unpack_kernel if not first else lambda *refs: unpack_kernel(*refs[:-1], None, refs[-1]),
            out_shape=jax.ShapeDtypeStruct((rows, vecs), trial.dtype),
            grid=(1,),
            in_specs=[SMEM, half] + whole + ([] if first else [ANY]),
            out_specs=half,
            input_output_aliases={} if first else {6: 0},
            name="unpack",
        )(live, base, share(0), got_near, got_inner, got_far, *([] if first else [sigma]))
    return sigma


def gathered(masked, factors, n_aux):
    everyone = lax.all_gather(masked, "pair", axis=0, tiled=True)
    rows = factors.reshape(-1, factors.shape[2])
    coeffs = exchange_sum(contract_rows(everyone, rows), n_aux)
    shares = lax.dot_general(
        rows, coeffs, (((1,), (1,)), ((), ())), preferred_element_type=jnp.float32
    )
    return lax.psum_scatter(
        shares.astype(jnp.bfloat16), "pair", scatter_dimension=0, tiled=True
    ).astype(jnp.float32)


def body(n_traj, n_pair, n_aux, b_built, trial, energy_gap, block_live):
    blocks = trial.shape[0] // BLK
    aux = lax.axis_index("aux")
    base = energy_gap[:, None] * trial.astype(jnp.float32)
    if n_pair == 4:
        groups = n_traj * n_pair
        sent = jnp.broadcast_to(block_live[None], (groups, block_live.shape[0]))
        everyone = lax.all_to_all(sent, ("traj", "pair"), 0, 0, tiled=True)
        counts = everyone.reshape(groups, n_aux, blocks).sum(axis=2)
        least = (blocks * 5) // 8
        which = jnp.clip(jnp.max(counts) - least, 0, blocks - least)
        me = lax.axis_index("pair")
        order = lax.axis_index("traj") * n_pair + (me ^ jnp.arange(n_pair))
        columns = aux * blocks + jnp.arange(blocks)
        live = everyone[order[:, None], columns[None, :]]
        return lax.switch(
            which,
            [functools.partial(along_line, slots, n_aux) for slots in range(least, blocks + 1)],
            live,
            trial,
            b_built[0],
            base,
        )
    own_blocks = lax.dynamic_slice_in_dim(block_live, aux * blocks, blocks, 0)
    own_live = jnp.repeat(own_blocks, BLK)
    masked = trial * own_live.astype(jnp.bfloat16)[:, None]
    response = gathered(masked, b_built[0], n_aux)
    return (base + 2.0 * own_live.astype(jnp.float32)[:, None] * response).astype(jnp.bfloat16)


def solution(mesh):
    sizes = [mesh.shape[axis] for axis in ("traj", "pair", "aux")]
    return jax.shard_map(
        functools.partial(body, *sizes),
        mesh=mesh,
        in_specs=(
            P(("traj", "aux"), None, None, "pair"),
            P(("traj", "pair", "aux"), "root"),
            P(("traj", "pair", "aux")),
            P(("traj", "pair")),
        ),
        out_specs=P(("traj", "pair", "aux"), "root"),
        check_vma=False,
    )
```

time: 94.5 us -> 183 us (1.94)
  Pallas kernels: 0 us -> 104 us
  waiting for transfers between devices: 43.3 us -> 17.4 us
  starting transfers between devices: 31.1 us -> 35.5 us
  other arithmetic: 2.94 us -> 6.12 us
    pallas_call x0 -> x4, Pallas kernels: none -> 104 us  [the longest x1 97.4 us: along_line(): pl.pallas_call(functools.partial(pack_factors_kernel, slots), out_shape=j...]
    ppermute x2, waiting for transfers between devices: 18.2 us -> 0.01 us  [along_line(): from_far = lax.ppermute(own, 'pair', far)]
    ppermute x2, waiting for transfers between devices: 8.01 us -> 0.01 us  [along_line(): got_near = lax.ppermute(share(1).astype(jnp.bfloat16), 'pair', near)]
    all_to_all x0 -> x1, starting transfers between devices: none -> 7.28 us  [body(): everyone = lax.all_to_all(sent, ('traj', 'pair'), 0, 0, tiled=True)]
    ppermute x2, starting transfers between devices: 7.31 us -> 0.8 us  [along_line(): from_far = lax.ppermute(own, 'pair', far)]
    all_to_all x0 -> x1, waiting for transfers between devices: none -> 4.18 us  [body(): everyone = lax.all_to_all(sent, ('traj', 'pair'), 0, 0, tiled=True)]
    ppermute x2, waiting for transfers between devices: 11.5 us -> 8.56 us  [along_line(): got_far = lax.ppermute(onward.astype(jnp.bfloat16), 'pair', far)]
    ppermute x2, starting transfers between devices: 1.58 us -> 4.15 us  [along_line(): from_near = lax.ppermute(own, 'pair', near)]
  transfers between devices with their start and end apart: 18 -> 19, of which waited for: 8 -> 7; matrix products, arithmetic and copies ran while one was open for 14% -> 11% of each run, Pallas kernels for 0% -> 55%
where the time goes in v3:
time: 183 us; the launch traced here: 182 us
  Pallas kernels  104 us (57%)
  starting transfers between devices  35.5 us (19%)
  waiting for transfers between devices  17.4 us (10%)
  matrix products  15.2 us (8%)
  other arithmetic  6.12 us (3%)
  local copies, waits for them, and re-layouts  3.32 us (2%)
    pallas_call x1, Pallas kernels, along_line(): pl.pallas_call(functools.partial(pack_factors_kernel, slots), out_shape=j...  97.4 us
    dot_general x8, matrix products, contract_rows(): lax.dot_general(left, right, (((0,), (0,)), ((), ())), preferred_element_...  8.72 us
    ppermute x2, waiting for transfers between devices, along_line(): got_far = lax.ppermute(onward.astype(jnp.bfloat16), 'pair', far)  8.56 us
    ppermute x2, starting transfers between devices, along_line(): got_outer = lax.ppermute(share_3, 'pair', inward)  8.13 us
    all_to_all x1, starting transfers between devices, body(): everyone = lax.all_to_all(sent, ('traj', 'pair'), 0, 0, tiled=True)  7.28 us
    dot_general x8, matrix products, share(): lax.dot_general(packed[flip], coeffs, (((1,), (1,)), ((), ())), preferred...  6.5 us
    pallas_call x2, Pallas kernels, along_line(): pl.pallas_call(unpack_kernel if not first else lambda *refs: unpack_kerne...  4.43 us
    all_to_all x1, waiting for transfers between devices, body(): everyone = lax.all_to_all(sent, ('traj', 'pair'), 0, 0, tiled=True)  4.18 us
  transfers between devices with their start and end apart: 19, of which 7 were waited for; matrix products, arithmetic and copies ran while one was open for 11% of the time, Pallas kernels for 55%

profile of v3, /device:TPU:0, one launch (start us, length us, event | category | flops | bytes accessed | tf_op | source)
XLA Modules:
  0.0 182.3 jit_solution(7769451396287595102)
XLA Ops:
  0.0 1.2 broadcast_in_dim.6
  1.2 7.3 %all-to-all-start = ((s32[8,1,16]{2,1,0:T(1,128)}), s32[8,1,16]{2,1,0:T(1,128)S(1)}, u32[]{:S(2)}, u32[]{:S(2)}) async-start(s32[8,1,16]{2,1,0:T(1,128)} %broadcast_in_dim.6), calls=%async_computation | async-start | bytes 8192 | tf_op jit(solution)/shard_map/all_to_all | solution.py:190
  8.6 0.1 broadcast_in_dim.7
  8.6 2.1 %convert_element_type.171 = f32[1024,256]{1,0:T(8,128)} convert(bf16[1024,256]{1,0:T(8,128)(2,1)} %param.9) | non-fusion elementwise | flops 262144 | bytes 1572864 | tf_op jit(solution)/shard_map/convert_element_type | solution.py:186
  10.7 4.2 %all-to-all-done = s32[8,1,16]{2,1,0:T(1,128)S(1)} async-done(((s32[8,1,16]{2,1,0:T(1,128)}), s32[8,1,16]{2,1,0:T(1,128)S(1)}, u32[]{:S(2)}, u32[]{:S(2)}) %all-to-all-start) | async-done | bytes 544 | tf_op jit(solution)/shard_map/all_to_all | solution.py:190
  14.9 0.5 broadcast.127
  15.4 0.7 reduce.3
  16.1 0.1 reshape.45
  16.2 0.2 reduce_sum.9
  16.4 0.6 reduce_max.9
  17.7 164.6 %conditional.1 = (bf16[1024,256]{1,0:T(8,128)(2,1)}) conditional(s32[]{:T(128)} %clamp.3, (s32[8,1,16]{2,1,0:T(1,128)S(1)}, bf16[1,4,1024,512]{3,2,1,0:T(8,128)(2,1)}, bf16[1024,256]{1,0:T(8,128)(2,1)}, f32[1024]{0:T(1024)}, s32[4,8,2]{1,0,2:T(4,128)S(1)}, /*index=5*/f32[1024,256]{1,0:T(8,128)}) %tuple.17, ...), branch_computations={%region_2.3_spmd, %region_3.4_spmd, %region_4.5_spmd, %region_5.6_... | conditional | flops 2150236160 | bytes 77879744 | solution.py:198
  17.7 0.1 reshape.52
  17.8 0.7 gather_fusion.1
  18.5 0.6 reshape.55.live_ref.refs_0_
  19.1 1.9 %pack_trial.5 = (bf16[768,128]{1,0:T(8,128)(2,1)}, bf16[768,128]{1,0:T(8,128)(2,1)}) custom-call(s32[4,8]{1,0:T(4,128)} %reshape.55.live_ref.refs_0_, bf16[1024,256]{1,0:T(8,128)(2,1)} %get-tuple-element.51.trial_ref), custom_call_target="tpu_custom_call" | custom-call | tf_op jit(solution)/shard_map/cond/branch_1_fun/pack_trial/pallas_call | solution.py:113
  21.1 0.6 collective-permute-start.27
  21.6 0.6 collective-permute-start.28
  22.2 1.3 collective-permute-start.29
  23.5 3.6 %collective-permute-start.18 = (bf16[768,128]{1,0:T(8,128)(2,1)}, bf16[768,128]{1,0:T(8,128)(2,1)}, u32[]{:S(2)}, u32[]{:S(2)}) collective-permute-start(bf16[768,128]{1,0:T(8,128)(2,1)} %get-tuple-element.52), channel_id=1, source_target_pairs={{0,4},{4,0},{8,12},{12,8},{1,5},{5,1},{9,13},{13,9},{2,6},{6,2},{1... | collective-permute-start | bytes 589832 | tf_op jit(solution)/shard_map/cond/branch_1_fun/ppermute | solution.py:135
  27.1 0.2 collective-permute-start.19
  27.3 97.4 %pack_factors.5 = bf16[4,768,512]{2,1,0:T(8,128)(2,1)} custom-call(s32[4,8]{1,0:T(4,128)} %reshape.55.live_ref.refs_0_, s32[1]{0:T(128)} %bitcast.10.me_ref, bf16[4,1024,512]{2,1,0:T(8,128)(2,1)} %bitcast.197), custom_call_target="tpu_custom_call" | custom-call | tf_op jit(solution)/shard_map/cond/branch_1_fun/pack_factors/pallas_call | solution.py:120
  124.8 1.7 fusion.13
  126.5 2.4 %broadcast_multiply_fusion.1.refs_1_.base_ref = f32[1024,256]{1,0:T(8,128)} fusion(f32[1024,256]{1,0:T(8,128)} %get-tuple-element.82, f32[1024]{0:T(1024)S(1)} %copy-done.32), kind=kLoop, calls=%fused_computation.52 | loop fusion | flops 262144 | bytes 2101248 | tf_op jit(solution)/shard_map/mul | solution.py:186
  128.9 1.5 fusion.15
  130.5 0.7 collective-permute-start.20
  131.1 0.0 collective-permute-done.28
  131.2 1.3 collective-permute-start.30
  132.5 1.3 collective-permute-start.21
  133.8 1.2 convolution_add_fusion.12
  135.0 1.2 convolution_add_fusion.11
  136.3 0.0 collective-permute-done.18
  136.3 1.2 convolution_add_fusion.15
  137.5 1.2 convolution_add_fusion.14
  138.7 2.3 %collective-permute-done.30 = bf16[768,128]{1,0:T(8,128)(2,1)S(1)} collective-permute-done((bf16[768,128]{1,0:T(8,128)(2,1)}, bf16[768,128]{1,0:T(8,128)(2,1)S(1)}, u32[]{:S(2)}, u32[]{:S(2)}) %collective-permute-start.30) | collective-permute-done | bytes 196640 | tf_op jit(solution)/shard_map/cond/branch_1_fun/ppermute | solution.py:137
  141.0 0.3 fusion.43
  141.3 1.6 collective-permute-start.31
  142.9 0.2 collective-permute-done.21
  143.1 0.3 fusion.42
  143.4 1.6 collective-permute-start.22
  145.0 1.4 collective-permute-done.31
  146.4 0.4 convolution_convert_fusion.4
  146.8 5.1 %collective-permute-start.34 = (bf16[768,128]{1,0:T(8,128)(2,1)S(1)}, bf16[768,128]{1,0:T(8,128)(2,1)S(1)}, u32[]{:S(2)}, u32[]{:S(2)}) collective-permute-start(bf16[768,128]{1,0:T(8,128)(2,1)S(1)} %convolution_convert_fusion.4), channel_id=1, source_target_pairs={{12,8},{0,4},{13,9},{1,5},{14,10},{2,6},{15,11},{3,7},{28,24},{16,... | collective-permute-start | bytes 589832 | tf_op jit(solution)/shard_map/cond/branch_1_fun/ppermute | solution.py:151
  151.9 0.7 collective-permute-start.33
  152.5 1.1 fusion.12.refs_2_
  153.7 0.4 convolution_convert_fusion.5
  154.0 0.0 collective-permute-done.22
  154.1 1.1 convolution_convert_fusion.6
  155.1 3.1 %collective-permute-start.25 = (bf16[768,128]{1,0:T(8,128)(2,1)}, bf16[768,128]{1,0:T(8,128)(2,1)S(1)}, u32[]{:S(2)}, u32[]{:S(2)}) collective-permute-start(bf16[768,128]{1,0:T(8,128)(2,1)} %convolution_convert_fusion.6), channel_id=1, source_target_pairs={{12,8},{0,4},{13,9},{1,5},{14,10},{2,6},{15,11},{3,7},{28,24},{16,... | collective-permute-start | bytes 589832 | tf_op jit(solution)/shard_map/cond/branch_1_fun/ppermute | solution.py:151
  158.2 1.4 collective-permute-start.24
  159.6 1.5 collective-permute-start.32
  161.0 1.0 convolution_convert_fusion.7
  162.1 0.0 collective-permute-done.34
  162.1 0.5 collective-permute-start.23
  162.6 0.4 fusion.11
  163.0 0.8 collective-permute-done.25
  163.8 3.3 %collective-permute-start.35 = (bf16[768,128]{1,0:T(8,128)(2,1)S(1)}, bf16[768,128]{1,0:T(8,128)(2,1)}, u32[]{:S(2)}, u32[]{:S(2)}) collective-permute-start(bf16[768,128]{1,0:T(8,128)(2,1)S(1)} %fusion.11), channel_id=1, source_target_pairs={{0,8},{4,12},{8,0},{12,4},{1,9},{5,13},{9,1},{13,5},{2,10},{6,14},... | collective-permute-start | bytes 589832 | tf_op jit(solution)/shard_map/cond/branch_1_fun/ppermute | solution.py:155
  167.1 1.0 fusion.10
  168.2 0.0 collective-permute-done.33.refs_4_
  168.2 0.0 collective-permute-start.26
  168.2 1.1 fusion.14.own_ref
  169.3 4.7 %collective-permute-done.35.refs_5_ = bf16[768,128]{1,0:T(8,128)(2,1)} collective-permute-done((bf16[768,128]{1,0:T(8,128)(2,1)S(1)}, bf16[768,128]{1,0:T(8,128)(2,1)}, u32[]{:S(2)}, u32[]{:S(2)}) %collective-permute-start.35) | collective-permute-done | bytes 196640 | tf_op jit(solution)/shard_map/cond/branch_1_fun/ppermute | solution.py:155
  174.0 2.2 %unpack.10.before_ref = bf16[1024,256]{1,0:T(8,128)(2,1)} custom-call(s32[4,8]{1,0:T(4,128)} %reshape.55.live_ref.refs_0_, f32[1024,256]{1,0:T(8,128)} %broadcast_multiply_fusion.1.refs_1_.base_ref, f32[768,128]{1,0:T(8,128)} %fusion.12.refs_2_, bf16[768,128]{1,0:T(8,128)(2,1)} %copy-done.23, bf16[768,128]{1,0:T(8,128)(2,1)} %copy-done.22, ...), custom_call_target="tpu_custom_call" | custom-call | tf_op jit(solution)/shard_map/cond/branch_1_fun/unpack/pallas_call | solution.py:159
  176.3 3.9 %collective-permute-done.26.far_ref = bf16[768,128]{1,0:T(8,128)(2,1)} collective-permute-done((bf16[768,128]{1,0:T(8,128)(2,1)}, bf16[768,128]{1,0:T(8,128)(2,1)}, u32[]{:S(2)}, u32[]{:S(2)}) %collective-permute-start.26) | collective-permute-done | bytes 196640 | tf_op jit(solution)/shard_map/cond/branch_1_fun/ppermute | solution.py:155
  180.1 2.2 %unpack.11 = bf16[1024,256]{1,0:T(8,128)(2,1)} custom-call(s32[4,8]{1,0:T(4,128)} %reshape.55.live_ref.refs_0_, f32[1024,256]{1,0:T(8,128)} %broadcast_multiply_fusion.1.refs_1_.base_ref, f32[768,128]{1,0:T(8,128)} %fusion.14.own_ref, bf16[768,128]{1,0:T(8,128)(2,1)} %collective-permute-done.23.near_ref, ...), custom_call_target="tpu_custom_call", output_to_operand_aliasing={{}: (6, {})} | custom-call | tf_op jit(solution)/shard_map/cond/branch_1_fun/unpack/pallas_call | solution.py:159
  (22 shorter events, 0.1 us)
Async XLA Ops:
  1.2 13.7 %all-to-all-start = ((s32[8,1,16]{2,1,0:T(1,128)}), s32[8,1,16]{2,1,0:T(1,128)S(1)}, u32[]{:S(2)}, u32[]{:S(2)}) async-start(s32[8,1,16]{2,1,0:T(1,128)} %broadcast_in_dim.6), calls=%async_computation | async-start | bytes 8192 | tf_op jit(solution)/shard_map/all_to_all | solution.py:190
  21.1 109.4 %collective-permute-start.27 = (bf16[768,128]{1,0:T(8,128)(2,1)}, bf16[768,128]{1,0:T(8,128)(2,1)}, u32[]{:S(2)}, u32[]{:S(2)}) collective-permute-start(bf16[768,128]{1,0:T(8,128)(2,1)} %get-tuple-element.53), channel_id=1, source_target_pairs={{0,4},{4,0},{8,12},{12,8},{1,5},{5,1},{9,13},{13,9},{2,6},{6,2},{1... | collective-permute-start | bytes 589832 | tf_op jit(solution)/shard_map/cond/branch_1_fun/ppermute | solution.py:135
  21.6 109.5 %collective-permute-start.28 = (bf16[768,128]{1,0:T(8,128)(2,1)}, bf16[768,128]{1,0:T(8,128)(2,1)}, u32[]{:S(2)}, u32[]{:S(2)}) collective-permute-start(bf16[768,128]{1,0:T(8,128)(2,1)} %get-tuple-element.53), channel_id=1, source_target_pairs={{0,8},{4,12},{8,0},{12,4},{1,9},{5,13},{9,1},{13,5},{2,10},{6,14},... | collective-permute-start | bytes 589832 | tf_op jit(solution)/shard_map/cond/branch_1_fun/ppermute | solution.py:134
  22.2 116.6 %collective-permute-start.29 = (bf16[768,128]{1,0:T(8,128)(2,1)}, bf16[768,128]{1,0:T(8,128)(2,1)}, u32[]{:S(2)}, u32[]{:S(2)}) collective-permute-start(bf16[768,128]{1,0:T(8,128)(2,1)} %get-tuple-element.53), channel_id=1, source_target_pairs={{4,8},{8,4},{5,9},{9,5},{6,10},{10,6},{7,11},{11,7},{20,24},{24,20... | collective-permute-start | bytes 589832 | tf_op jit(solution)/shard_map/cond/branch_1_fun/ppermute | solution.py:136
  23.5 112.7 %collective-permute-start.18 = (bf16[768,128]{1,0:T(8,128)(2,1)}, bf16[768,128]{1,0:T(8,128)(2,1)}, u32[]{:S(2)}, u32[]{:S(2)}) collective-permute-start(bf16[768,128]{1,0:T(8,128)(2,1)} %get-tuple-element.52), channel_id=1, source_target_pairs={{0,4},{4,0},{8,12},{12,8},{1,5},{5,1},{9,13},{13,9},{2,6},{6,2},{1... | collective-permute-start | bytes 589832 | tf_op jit(solution)/shard_map/cond/branch_1_fun/ppermute | solution.py:135
  27.1 105.4 %collective-permute-start.19 = (bf16[768,128]{1,0:T(8,128)(2,1)}, bf16[768,128]{1,0:T(8,128)(2,1)}, u32[]{:S(2)}, u32[]{:S(2)}) collective-permute-start(bf16[768,128]{1,0:T(8,128)(2,1)} %get-tuple-element.52), channel_id=1, source_target_pairs={{0,8},{4,12},{8,0},{12,4},{1,9},{5,13},{9,1},{13,5},{2,10},{6,14},... | collective-permute-start | bytes 589832 | tf_op jit(solution)/shard_map/cond/branch_1_fun/ppermute | solution.py:134
  27.3 99.1 %copy-start.32 = (f32[1024]{0:T(1024)S(1)}, f32[1024]{0:T(1024)}, u32[]{:S(2)}) copy-start(f32[1024]{0:T(1024)} %get-tuple-element.108) | copy-start | bytes 12292 | tf_op jit(solution)/shard_map/cond
  124.8 9.0 %copy-start.2 = (bf16[4,768,512]{2,1,0:T(8,128)(2,1)S(1)}, bf16[4,768,512]{2,1,0:T(8,128)(2,1)}, u32[]{:S(2)}) copy-start(bf16[4,768,512]{2,1,0:T(8,128)(2,1)} %pack_factors.5) | copy-start | bytes 9437188 | tf_op jit(solution)/shard_map/cond
  130.5 12.4 %collective-permute-start.20 = (bf16[768,128]{1,0:T(8,128)(2,1)}, bf16[768,128]{1,0:T(8,128)(2,1)S(1)}, u32[]{:S(2)}, u32[]{:S(2)}) collective-permute-start(bf16[768,128]{1,0:T(8,128)(2,1)} %get-tuple-element.52), channel_id=1, source_target_pairs={{4,8},{8,4},{5,9},{9,5},{6,10},{10,6},{7,11},{11,7},{20,24},{24,20... | collective-permute-start | bytes 589832 | tf_op jit(solution)/shard_map/cond/branch_1_fun/ppermute | solution.py:136
  131.2 9.9 %collective-permute-start.30 = (bf16[768,128]{1,0:T(8,128)(2,1)}, bf16[768,128]{1,0:T(8,128)(2,1)S(1)}, u32[]{:S(2)}, u32[]{:S(2)}) collective-permute-start(bf16[768,128]{1,0:T(8,128)(2,1)} %collective-permute-done.28), channel_id=1, source_target_pairs={{8,12},{4,0},{9,13},{5,1},{10,14},{6,2},{11,15},{7,3},{24,28},{20,... | collective-permute-start | bytes 589832 | tf_op jit(solution)/shard_map/cond/branch_1_fun/ppermute | solution.py:137
  132.5 10.7 %collective-permute-start.21 = (bf16[768,128]{1,0:T(8,128)(2,1)}, bf16[768,128]{1,0:T(8,128)(2,1)S(1)}, u32[]{:S(2)}, u32[]{:S(2)}) collective-permute-start(bf16[768,128]{1,0:T(8,128)(2,1)} %collective-permute-done.19), channel_id=1, source_target_pairs={{8,12},{4,0},{9,13},{5,1},{10,14},{6,2},{11,15},{7,3},{24,28},{20,... | collective-permute-start | bytes 589832 | tf_op jit(solution)/shard_map/cond/branch_1_fun/ppermute | solution.py:137
  141.3 5.0 %collective-permute-start.31 = (bf16[128,512]{1,0:T(8,128)(2,1)S(1)}, bf16[128,512]{1,0:T(8,128)(2,1)S(1)}, u32[]{:S(2)}, u32[]{:S(2)}) collective-permute-start(bf16[128,512]{1,0:T(8,128)(2,1)S(1)} %get-tuple-element.189), channel_id=1, source_target_pairs={{0,2},{2,0},{1,3},{3,1},{4,6},{6,4},{5,7},{7,5},{8,10},{10,8},{9,1... | collective-permute-start | bytes 393224 | tf_op jit(solution)/shard_map/cond/branch_1_fun/ppermute | solution.py:29
  143.4 10.6 %collective-permute-start.22 = (bf16[128,512]{1,0:T(8,128)(2,1)S(1)}, bf16[128,512]{1,0:T(8,128)(2,1)S(1)}, u32[]{:S(2)}, u32[]{:S(2)}) collective-permute-start(bf16[128,512]{1,0:T(8,128)(2,1)S(1)} %get-tuple-element.187), channel_id=1, source_target_pairs={{0,2},{2,0},{1,3},{3,1},{4,6},{6,4},{5,7},{7,5},{8,10},{10,8},{9,1... | collective-permute-start | bytes 393224 | tf_op jit(solution)/shard_map/cond/branch_1_fun/ppermute | solution.py:29
  146.8 15.3 %collective-permute-start.34 = (bf16[768,128]{1,0:T(8,128)(2,1)S(1)}, bf16[768,128]{1,0:T(8,128)(2,1)S(1)}, u32[]{:S(2)}, u32[]{:S(2)}) collective-permute-start(bf16[768,128]{1,0:T(8,128)(2,1)S(1)} %convolution_convert_fusion.4), channel_id=1, source_target_pairs={{12,8},{0,4},{13,9},{1,5},{14,10},{2,6},{15,11},{3,7},{28,24},{16,... | collective-permute-start | bytes 589832 | tf_op jit(solution)/shard_map/cond/branch_1_fun/ppermute | solution.py:151
  151.9 16.3 %collective-permute-start.33 = (bf16[768,128]{1,0:T(8,128)(2,1)S(1)}, bf16[768,128]{1,0:T(8,128)(2,1)S(1)}, u32[]{:S(2)}, u32[]{:S(2)}) collective-permute-start(bf16[768,128]{1,0:T(8,128)(2,1)S(1)} %convolution_convert_fusion.4), channel_id=1, source_target_pairs={{4,8},{8,4},{5,9},{9,5},{6,10},{10,6},{7,11},{11,7},{20,24},{24,20... | collective-permute-start | bytes 589832 | tf_op jit(solution)/shard_map/cond/branch_1_fun/ppermute | solution.py:152
  155.1 8.7 %collective-permute-start.25 = (bf16[768,128]{1,0:T(8,128)(2,1)}, bf16[768,128]{1,0:T(8,128)(2,1)S(1)}, u32[]{:S(2)}, u32[]{:S(2)}) collective-permute-start(bf16[768,128]{1,0:T(8,128)(2,1)} %convolution_convert_fusion.6), channel_id=1, source_target_pairs={{12,8},{0,4},{13,9},{1,5},{14,10},{2,6},{15,11},{3,7},{28,24},{16,... | collective-permute-start | bytes 589832 | tf_op jit(solution)/shard_map/cond/branch_1_fun/ppermute | solution.py:151
  158.2 18.0 %collective-permute-start.24 = (bf16[768,128]{1,0:T(8,128)(2,1)}, bf16[768,128]{1,0:T(8,128)(2,1)}, u32[]{:S(2)}, u32[]{:S(2)}) collective-permute-start(bf16[768,128]{1,0:T(8,128)(2,1)} %convolution_convert_fusion.6), channel_id=1, source_target_pairs={{4,8},{8,4},{5,9},{9,5},{6,10},{10,6},{7,11},{11,7},{20,24},{24,20... | collective-permute-start | bytes 589832 | tf_op jit(solution)/shard_map/cond/branch_1_fun/ppermute | solution.py:152
  159.6 9.8 %collective-permute-start.32 = (bf16[768,128]{1,0:T(8,128)(2,1)S(1)}, bf16[768,128]{1,0:T(8,128)(2,1)S(1)}, u32[]{:S(2)}, u32[]{:S(2)}) collective-permute-start(bf16[768,128]{1,0:T(8,128)(2,1)S(1)} %convolution_convert_fusion.5), channel_id=1, source_target_pairs={{0,4},{4,0},{8,12},{12,8},{1,5},{5,1},{9,13},{13,9},{2,6},{6,2},{1... | collective-permute-start | bytes 589832 | tf_op jit(solution)/shard_map/cond/branch_1_fun/ppermute | solution.py:153
  162.1 14.2 %collective-permute-start.23 = (bf16[768,128]{1,0:T(8,128)(2,1)}, bf16[768,128]{1,0:T(8,128)(2,1)}, u32[]{:S(2)}, u32[]{:S(2)}) collective-permute-start(bf16[768,128]{1,0:T(8,128)(2,1)} %convolution_convert_fusion.7), channel_id=1, source_target_pairs={{0,4},{4,0},{8,12},{12,8},{1,5},{5,1},{9,13},{13,9},{2,6},{6,2},{1... | collective-permute-start | bytes 589832 | tf_op jit(solution)/shard_map/cond/branch_1_fun/ppermute | solution.py:153
  163.8 10.2 %collective-permute-start.35 = (bf16[768,128]{1,0:T(8,128)(2,1)S(1)}, bf16[768,128]{1,0:T(8,128)(2,1)}, u32[]{:S(2)}, u32[]{:S(2)}) collective-permute-start(bf16[768,128]{1,0:T(8,128)(2,1)S(1)} %fusion.11), channel_id=1, source_target_pairs={{0,8},{4,12},{8,0},{12,4},{1,9},{5,13},{9,1},{13,5},{2,10},{6,14},... | collective-permute-start | bytes 589832 | tf_op jit(solution)/shard_map/cond/branch_1_fun/ppermute | solution.py:155
  168.2 5.8 %copy-start.22 = (bf16[768,128]{1,0:T(8,128)(2,1)}, bf16[768,128]{1,0:T(8,128)(2,1)S(1)}, u32[]{:S(2)}) copy-start(bf16[768,128]{1,0:T(8,128)(2,1)S(1)} %collective-permute-done.33.refs_4_) | copy-start | bytes 589828 | tf_op jit(solution)/shard_map/cond
  168.2 11.9 %collective-permute-start.26 = (bf16[768,128]{1,0:T(8,128)(2,1)}, bf16[768,128]{1,0:T(8,128)(2,1)}, u32[]{:S(2)}, u32[]{:S(2)}) collective-permute-start(bf16[768,128]{1,0:T(8,128)(2,1)} %fusion.10), channel_id=1, source_target_pairs={{0,8},{4,12},{8,0},{12,4},{1,9},{5,13},{9,1},{13,5},{2,10},{6,14},... | collective-permute-start | bytes 589832 | tf_op jit(solution)/shard_map/cond/branch_1_fun/ppermute | solution.py:155
  169.3 4.7 %copy-start.23 = (bf16[768,128]{1,0:T(8,128)(2,1)}, bf16[768,128]{1,0:T(8,128)(2,1)S(1)}, u32[]{:S(2)}) copy-start(bf16[768,128]{1,0:T(8,128)(2,1)S(1)} %collective-permute-done.32.refs_3_) | copy-start | bytes 589828 | tf_op jit(solution)/shard_map/cond
